TPU v7x, 32 devices: a whole 2x2x4 slice. The times are simulated.
32 devices in a mesh: replica: 8 (over z, core), tensor: 4 (over y, x).
Axes of the slice: x: 2, y: 2, z: 4, core: 2. Of those that a mesh axis runs over, the one named last changes fastest.
Arguments:
- tokens: bfloat16 [4096, 1024], P('replica'), may hold values from -6 to 6
- targets: bfloat16 [4096, 1024], P('replica'), may hold values from -6 to 6
- row_ids: int32 [8, 3, 512], P('replica'), may hold values from 0 to 511
- anchor: float32 [2, 1024, 4096], P(None, None, 'tensor'), may hold values from -0.1875 to 0.1875
- momentum: float32 [8, 2, 1024, 4096], P('replica', None, None, 'tensor'), may hold values from -4 to 4
- slow: float32 [2, 1024, 4096], P(None, None, 'tensor'), may hold values from -6 to 6
Outputs:
- anchor_new: float32 [2, 1024, 4096], P(None, None, 'tensor')
- slow_new: float32 [2, 1024, 4096], P(None, None, 'tensor')
- momentum_new: float32 [8, 2, 1024, 4096], P('replica', None, None, 'tensor')
Inputs may be any that keep to these rules, and one draw needn't show every extreme that they name: `row_ids`: each id names a row within its replica's own block of 512 rows; rows may repeat.
All inputs are finite; a program needn't handle non-finite values.
Results may differ from a plain program's by a relative error of at most 0.008.
Values may be sent and summed in bfloat16 or wider, within the bound.
No kernel may reach another device: no remote copies, remote signals or barrier semaphores. Data moves between devices by JAX's collectives and lax.ppermute only.
A program may use at most 128 MiB of HBM per device.

v0:
```python
import functools

import jax
import jax.numpy as jnp
from jax import lax
from jax.experimental import pallas as pl
from jax.experimental.pallas import tpu as pltpu
from jax.sharding import PartitionSpec as P

INNER = 3


learn_rate = 0.02
inner_beta = 0.9
slow_beta = 0.5
chunks = 4
bf16, f32 = jnp.bfloat16, jnp.float32
ANY = pl.BlockSpec(memory_space=pl.ANY)
LIGHT = pl.CostEstimate(flops=1, bytes_accessed=1, transcendentals=0)


def swapped(block, axis, mask):
    return lax.ppermute(block, axis, [(i, i ^ mask) for i in range(lax.axis_size(axis))])


def gelu_pair(pre):
    coeff = 0.7978845608028654
    square = pre * pre
    tanh_val = jnp.tanh(coeff * (pre + 0.044715 * square * pre))
    half = 0.5 * (1.0 + tanh_val)
    slope = half + 0.5 * pre * (1.0 - tanh_val * tanh_val) * coeff * (1.0 + 3.0 * 0.044715 * square)
    return (pre * half, slope)


def whole(shape):
    return pl.BlockSpec(shape, lambda j: (0,) * len(shape))


def loaded(state, k):
    if type(state) is not tuple:
        return state[k].astype(f32)
    each = len(state) // 2
    return jnp.concatenate([piece[...].astype(f32) for piece in state[k * each : (k + 1) * each]], axis=0)


def regrouped(refs, counts):
    refs, states = list(refs), []
    for count in counts:
        states.append(tuple(refs[:count]) if count > 1 else refs[0])
        del refs[:count]
    return states, refs


def flattened(states):
    flat = [state if type(state) is tuple else (state,) for state in states]
    return [len(state) for state in flat], [part for state in flat for part in state]


def block_of(part, block, parts=2):
    if part.ndim == 2:
        return pl.BlockSpec((part.shape[0], block), lambda j: (0, j))
    return pl.BlockSpec((parts, part.shape[1], block), lambda j: (0, 0, j))


def joined(pieces, place):
    if len(pieces) == 1:
        return pieces[0]

    @pl.when(pl.program_id(0) == 0)
    def _():
        size = pieces[0].shape[0]
        for b, piece in enumerate(pieces):
            place[b * size : (b + 1) * size] = piece[...]

    return place


def forward_kernel(mix, taken, pieces, waits, sums, emits, flag, *refs):
    rows, refs = refs[:pieces], refs[pieces:]
    sources, refs = regrouped(refs, taken)
    refs = refs[waits:]
    hidden, slope = refs[:2]
    inputs = joined(rows, refs[-1])
    block = [mix(flag[0], *[loaded(source, k) for source in sources]).astype(bf16) for k in range(2 if sums or emits else 1)]
    if emits:
        for k in range(2):
            refs[2 + sums][k] = block[k]
    j = pl.program_id(0)
    value, slope_val = gelu_pair(jnp.dot(inputs[...], block[0], preferred_element_type=f32))
    value = value.astype(bf16)
    hidden[...] = value
    slope[...] = slope_val.astype(bf16)
    if sums:
        partials, total = refs[2 : 2 + sums], refs[-2]
        out = lax.dot_general(value, block[1], (((1,), (1,)), ((), ())), preferred_element_type=f32)

        @pl.when(j == 0)
        def _():
            total[...] = out

        @pl.when(j > 0)
        def _():
            total[...] += out

        @pl.when(j == pl.num_programs(0) - 1)
        def _():
            size = partials[0].shape[0]
            for b, partial in enumerate(partials):
                partial[...] = total[b * size : (b + 1) * size].astype(bf16)


def forward(flag, inputs, sources, mix, sums, emits=True, waits=()):
    count, width = inputs[0].shape
    rows = count * len(inputs)
    units = sources[0].shape[2]
    block = min(units, 512)
    parts = 2 if sums or emits else 1
    counts, flat = flattened(sources)
    unit_spec = pl.BlockSpec((rows, block), lambda j: (0, j))
    shapes = [((rows, units), unit_spec), ((rows, units), unit_spec)]
    if sums:
        shapes += [((rows // sums, width), whole((rows // sums, width)))] * sums
    shapes += [(sources[0].shape, block_of(sources[0], block))] * emits
    return pl.pallas_call(
        functools.partial(forward_kernel, mix, counts, len(inputs), len(waits), sums, emits),
        grid=(units // block,),
        in_specs=[pl.BlockSpec(memory_space=pltpu.SMEM)]
        + [whole(piece.shape) for piece in inputs]
        + [block_of(part, block, parts) for part in flat]
        + [ANY] * len(waits),
        out_specs=[spec for _, spec in shapes],
        out_shape=[jax.ShapeDtypeStruct(shape, bf16) for shape, _ in shapes],
        scratch_shapes=[pltpu.VMEM((rows, width), f32)] * bool(sums) + [pltpu.VMEM((rows, width), bf16)],
        compiler_params=pltpu.CompilerParams(vmem_limit_bytes=56 << 20),
        cost_estimate=LIGHT,
    )(flag, *inputs, *flat, *waits)


def only(flag, weights):
    return weights


def pushed(flag, weights, first, second):
    return weights - 0.5 * learn_rate * (first + second)


def halved(flag, found, weights, sent):
    return 0.5 * (weights + jnp.where(flag == 0, sent, found))


def backward_kernel(update, taken, pieces, given, by_core, flag, weights, slope, hidden, *refs):
    states, refs = regrouped(refs, taken)
    error_count, input_count = pieces
    errors, inputs = refs[:error_count], refs[error_count : error_count + input_count]
    error, error_t, rows, inputs_t = refs[-4:]
    refs = refs[error_count + input_count : -4]
    results, _ = regrouped(refs[len(refs) - sum(given) :], given)
    error, rows = joined(errors, error), joined(inputs, rows)

    @pl.when(pl.program_id(0) == 0)
    def _():
        error_t[...] = error[...].T
        inputs_t[...] = rows[...].T

    back = jnp.dot(error[...], weights[0].astype(bf16), preferred_element_type=f32) * slope[...].astype(f32)
    for k, (left, right) in enumerate(((inputs_t[...], back.astype(bf16)), (error_t[...], hidden[...]))):
        grad = jnp.dot(left, right, preferred_element_type=f32)
        values = update(grad, *[loaded(state, k) for state in states])
        for result, apart, value in zip(results, by_core, values):
            if type(result) is not tuple:
                result[k] = value.astype(result.dtype)
                continue
            if apart:
                for place, piece in enumerate(result):

                    @pl.when((flag[0] == k) == (place == 0))
                    def _():
                        piece[...] = value.astype(piece.dtype)

                continue
            each = len(result) // 2
            for i, piece in enumerate(result[k * each : (k + 1) * each]):
                size = piece.shape[0]
                piece[...] = value[i * size : (i + 1) * size].astype(piece.dtype)


def backward(flag, errors, weights, slope, hidden, inputs, states, update, kinds, waits=()):
    rows, width = hidden.shape[0], weights.shape[1]
    units = weights.shape[2]
    block = min(units, 512)
    counts, flat = flattened(states)
    kinds = [kind if type(kind) is tuple else (kind, 1) for kind in kinds]
    by_core = [count == "core" for _, count in kinds]
    kinds = [(kind, 2 if apart else count) for (kind, count), apart in zip(kinds, by_core)]
    shapes = []
    for kind, count in kinds:
        shape = weights.shape if count == 1 else (2 * width // count, units)
        shapes += [jax.ShapeDtypeStruct(shape, kind)] * count
    results = pl.pallas_call(
        functools.partial(
            backward_kernel, update, counts, (len(errors), len(inputs)), [count for _, count in kinds], by_core
        ),
        grid=(units // block,),
        in_specs=[
            pl.BlockSpec(memory_space=pltpu.SMEM),
            pl.BlockSpec((1, width, block), lambda j: (1, 0, j)),
            pl.BlockSpec((rows, block), lambda j: (0, j)),
            pl.BlockSpec((rows, block), lambda j: (0, j)),
        ]
        + [block_of(part, block) for part in flat]
        + [whole(piece.shape) for piece in (*errors, *inputs)]
        + [ANY] * len(waits),
        out_specs=[block_of(shape, block) for shape in shapes],
        out_shape=shapes,
        scratch_shapes=[pltpu.VMEM((rows, width), bf16), pltpu.VMEM((width, rows), bf16)] * 2,
        compiler_params=pltpu.CompilerParams(vmem_limit_bytes=56 << 20),
        cost_estimate=LIGHT,
    )(flag, weights, slope, hidden, *flat, *errors, *inputs, *waits)
    return regrouped(results, [count for _, count in kinds])[0]


def first_update(grad, moment):
    moment = inner_beta * moment + grad
    return (moment, moment)


def first_beside(grad, moment, own_moment, weights):
    moment = inner_beta * moment + grad
    return (moment, weights - 0.5 * learn_rate * (own_moment + moment))


def second_update(grad, moment, weights):
    moment_new = inner_beta * moment + grad
    return (moment_new, weights - learn_rate * moment_new, moment + (1.0 + inner_beta) * moment_new)


def second_beside(grad, moment, weights):
    return (weights - learn_rate * (inner_beta * moment + grad),)


def third_update(grad, moment, known):
    return (inner_beta * moment + grad, known + grad)


def rounded(value):
    return lax.reduce_precision(value, 8, 7).astype(bf16)


def added(left, right):
    return rounded(left.astype(f32) + right.astype(f32))


def nothing(*refs):
    pass


def tied(waits, block):
    return pl.pallas_call(
        nothing,
        in_specs=[ANY] * (1 + len(waits)),
        out_specs=ANY,
        out_shape=jax.ShapeDtypeStruct(block.shape, block.dtype),
        input_output_aliases={0: 0},
        cost_estimate=LIGHT,
    )(block, *waits)


def finish_kernel(replicas, flag, slow, anchor, own, theirs, *refs):
    anchor_new, slow_new, token = refs[-3:]
    for k in range(2):
        total = jnp.where(flag[0] == k, own[...].astype(f32), theirs[...].astype(f32))
        value = slow_beta * slow[k] + total / replicas
        slow_new[k] = value
        anchor_new[k] = anchor[k] - learn_rate * value
    token[...] = jnp.zeros_like(token)


def finish(flag, replicas, slow, anchor, own, theirs, position, before):
    size, units = own.shape
    steps = 2
    rows = pl.BlockSpec((2, size // steps, units), lambda j: (0, position * steps + j, 0))
    part = pl.BlockSpec((size // steps, units), lambda j: (j, 0))
    shape = jax.ShapeDtypeStruct(slow.shape, f32)
    return pl.pallas_call(
        functools.partial(finish_kernel, replicas),
        grid=(steps,),
        in_specs=[pl.BlockSpec(memory_space=pltpu.SMEM), rows, rows, part, part] + [ANY] * len(before),
        out_specs=[rows, rows, whole((8, 128))],
        out_shape=[shape, shape, jax.ShapeDtypeStruct((8, 128), bf16)],
        input_output_aliases={5 + k: k for k in range(len(before))},
        compiler_params=pltpu.CompilerParams(vmem_limit_bytes=60 << 20),
        cost_estimate=LIGHT,
    )(flag, slow, anchor, own, theirs, *before)


def slow_step(flag, mine, other, slow, anchor):
    axis, cores = "replica", 2
    index = lax.axis_index(axis)
    replicas = lax.axis_size(axis)
    chip = index // cores
    length = replicas // cores
    half = length // 2
    rows = mine.shape[0]
    size = rows // chunks

    def moved(part, hops):
        return lax.ppermute(part, axis, [(cores * a + c, cores * b + c) for a, b in hops for c in range(cores)])

    def at(places):
        return functools.reduce(jnp.logical_or, [chip == place for place in places])

    stages = [(True, [(s, s + 1), (length - 1 - s, length - 2 - s)]) for s in range(half - 1)]
    if half:
        stages.append((True, [(half - 1, half), (half, half - 1)]))
    stages += [(False, [(s + 1, s), (length - 2 - s, length - 1 - s)]) for s in reversed(range(half - 1))]

    pair_rows = rows // 2
    pairs = [swapped(other[p * pair_rows : (p + 1) * pair_rows], axis, 1) for p in range(2)]
    blocks = []
    for c in range(chunks):
        p, start = divmod(c * size, pair_rows)
        blocks.append(added(mine[c * size : (c + 1) * size], pairs[p][start : start + size]))
    arrived, made, results, tokens = {}, {}, [], []
    final = len(stages) - 1
    for tick in range(chunks + len(stages)):
        for s in reversed(range(len(stages) + 1)):
            c = tick - s
            if not 0 <= c < chunks:
                continue
            block = blocks[c]
            if s:
                adds, hops = stages[s - 1]
                fresh = added(block, arrived[s - 1, c]) if adds else arrived[s - 1, c]
                block = jnp.where(at([b for _, b in hops]), fresh, block)
                if s > final and 0 < c < chunks - 1:
                    block = tied([tokens[c - 1]], block)
            if s == 0 and c >= 3 and (2, c - 3) in made:
                block = tied([made[2, c - 3]], block)
            blocks[c] = made[s, c] = block
            if s < len(stages):
                arrived[s, c] = moved(block, stages[s][1])
            else:
                theirs = swapped(block, axis, 1)
                *results, token = finish(flag, replicas, slow, anchor, block, theirs, c, results)
                tokens.append(token)
    return results


def body(tokens, targets, row_ids, anchor, momentum, slow):
    row_count = tokens.shape[0]
    scale = 1.0 / row_count
    tensors = lax.axis_size("tensor")
    share_rows = row_count // tensors
    order = lax.axis_index("tensor") ^ jnp.arange(tensors)
    picks_all = row_ids[0].reshape(INNER, tensors, share_rows)[:, order].reshape(INNER, row_count)

    replicas = lax.axis_size("replica")
    flag = (lax.axis_index("replica") % 2).astype(jnp.int32).reshape(1)

    def gathered(own):
        return [own] + [swapped(own, "tensor", m) for m in range(1, tensors)]

    def error_share(partials, step):
        wanted = targets.at[picks_all[step, :share_rows]].get(mode="promise_in_bounds")
        share = partials[0].astype(f32)
        for m in range(1, tensors):
            share = share + swapped(partials[m], "tensor", m).astype(f32)
        return ((share - wanted.astype(f32)) * scale).astype(bf16)

    def sent(block, distance, which=(0, 1)):
        route = [((i - distance) % replicas, i) for i in range(replicas) if i % 2 in which]
        return lax.ppermute(block, "replica", route)

    def picked(step, count):
        return tokens.at[picks_all[step, :count]].get(mode="promise_in_bounds")

    near_share = sent(picked(0, share_rows), 1)
    narrow = tied([near_share], momentum[0].astype(bf16))
    moment_near = sent(narrow, 1)

    inputs = [picked(0, row_count)]
    hidden, slope, *partials = forward(flag, inputs, [anchor], only, tensors, emits=False, waits=[narrow])
    error = jnp.concatenate(gathered(error_share(partials, 0)))
    error_near = sent(error, 1)
    moment, moment_bf = backward(
        flag,
        [error],
        anchor,
        slope,
        hidden,
        inputs,
        [momentum[0]],
        first_update,
        [f32, (bf16, 2)],
    )
    inputs_near = gathered(near_share)
    hidden_near, slope_near = forward(flag, inputs_near, [anchor], only, 0, emits=False, waits=[moment])
    moment_far = [sent(tied([error_near, hidden_near], part), 2, (0,)) for part in moment_bf]
    moment_near, weights = backward(
        flag,
        [error_near],
        anchor,
        slope_near,
        hidden_near,
        inputs_near,
        [moment_near, moment, anchor],
        first_beside,
        [(bf16, 2), bf16],
    )

    inputs = [tied([moment_near[0]], picked(1, row_count))]
    inputs_far = sent(inputs[0], 2, (1,))
    hidden, slope, *partials = forward(flag, inputs, [weights], only, tensors, emits=False)
    error = jnp.concatenate(gathered(error_share(partials, 1)))
    error_far = sent(error, 2, (1,))
    moment, weights, known = backward(
        flag,
        [error],
        weights,
        slope,
        hidden,
        inputs,
        [moment, weights],
        second_update,
        [f32, bf16, bf16],
        waits=moment_far,
    )
    weights = tied([error_far, inputs_far], weights)
    weights_sent = sent(weights, 2, (0,))
    moment_two = tuple(sent(tied([weights], part), 1, (1,)) for part in moment_near)
    moment_three = tuple(sent(tied([weights], part), 1, (1,)) for part in moment_far)
    hidden, slope, weights_far = forward(flag, [inputs_far], [anchor, moment_two, moment_three], pushed, 0)
    (weights_found,) = backward(
        flag, [error_far], weights_far, slope, hidden, [inputs_far], [moment_two, weights_far], second_beside, [bf16]
    )

    inputs = [picked(2, row_count)]
    hidden, slope, *rest = forward(flag, inputs, [weights_found, weights, weights_sent], halved, tensors)
    errors = gathered(error_share(rest[:tensors], 2))
    moment, total = backward(
        flag, errors, rest[tensors], slope, hidden, inputs, [moment, known], third_update, [f32, (bf16, "core")]
    )
    anchor_new, slow_new = slow_step(flag, *total, slow, anchor)
    return (anchor_new, slow_new, moment[None])


def solution(mesh):
    return jax.shard_map(
        body,
        mesh=mesh,
        in_specs=(
            P("replica", None),
            P("replica", None),
            P("replica", None, None),
            P(None, None, "tensor"),
            P("replica", None, None, "tensor"),
            P(None, None, "tensor"),
        ),
        out_specs=(
            P(None, None, "tensor"),
            P(None, None, "tensor"),
            P("replica", None, None, "tensor"),
        ),
        check_vma=False,
    )
```

profile of v0, /device:TPU:0, one launch (start us, length us, event | category | flops | bytes accessed | tf_op | source)
XLA Modules:
  0.0 366.2 jit_solution(11954605959084131437)
XLA Ops:
  3.4 6.1 %bitcast_convert_fusion.refs_0_ = bf16[2,1024,1024]{2,1,0:T(8,128)(2,1)} fusion(f32[1,2,1024,1024]{3,2,1,0:T(8,128)} %param.10), kind=kLoop, calls=%fused_computation.61 | loop fusion | flops 2097152 | bytes 12582912 | tf_op jit(solution)/shard_map/convert_element_type | solution.py:378
  15.7 8.9 %shard_map.86 = (bf16[512,1024]{1,0:T(8,128)(2,1)}, bf16[512,1024]{1,0:T(8,128)(2,1)}, bf16[128,1024]{1,0:T(8,128)(2,1)}, bf16[128,1024]{1,0:T(8,128)(2,1)}, bf1...) custom-call(s32[1]{0:T(128)} %bitcast.flag, bf16[512,1024]{1,0:T(8,128)(2,1)} %gather_fusion.4, ...), custom_call_target="tpu_custom_call" | custom-call | flops 1 | bytes 1 | tf_op jit(solution)/shard_map/pallas_call | solution.py:124
  34.1 5.9 %collective-permute-done.5 = bf16[128,1024]{1,0:T(8,128)(2,1)S(1)} collective-permute-done((bf16[128,1024]{1,0:T(8,128)(2,1)}, bf16[128,1024]{1,0:T(8,128)(2,1)S(1)}, u32[]{:S(2)}, u32[]{:S(2)}) %collective-permute-start.5) | collective-permute-done | bytes 262176 | tf_op jit(solution)/shard_map/ppermute | solution.py:23
  45.5 6.7 %collective-permute-done.9 = bf16[128,1024]{1,0:T(8,128)(2,1)S(1)} collective-permute-done((bf16[128,1024]{1,0:T(8,128)(2,1)S(1)}, bf16[128,1024]{1,0:T(8,128)(2,1)S(1)}, u32[]{:S(2)}, u32[]{:S(2)}) %collective-permute-start.9) | collective-permute-done | bytes 262176 | tf_op jit(solution)/shard_map/ppermute | solution.py:23
  58.8 10.6 %shard_map.87 = (f32[2,1024,1024]{2,1,0:T(8,128)}, bf16[1024,1024]{1,0:T(8,128)(2,1)}, bf16[1024,1024]{1,0:T(8,128)(2,1)}) custom-call(s32[1]{0:T(128)} %bitcast.flag, f32[2,1024,1024]{2,1,0:T(8,128)} %anchor.7, bf16[512,1024]{1,0:T(8,128)(2,1)} %get-tuple-element.49.slope, bf16[512,1024]{1,0:T(8,128)(2,1)} %get-tuple-element.50.hidden, ...), custom_call_target="tpu_custom_call" | custom-call | flops 1 | bytes 1 | tf_op jit(solution)/shard_map/pallas_call | solution.py:199
  71.8 5.4 %shard_map.88 = (bf16[512,1024]{1,0:T(8,128)(2,1)}, bf16[512,1024]{1,0:T(8,128)(2,1)}) custom-call(s32[1]{0:T(128)} %bitcast.flag, bf16[128,1024]{1,0:T(8,128)(2,1)} %copy-done.11, bf16[128,1024]{1,0:T(8,128)(2,1)} %copy-done.18, bf16[128,1024]{1,0:T(8,128)(2,1)} %copy-done.17, bf16[128,1024]{1,0:T(8,128)(2,1)} %copy-done.16, f32[2,1024,1024]{2,1,0:T(8,128)} %anchor.7, ...), custom_call_target="tpu_custom_call" | custom-call | flops 1 | bytes 1 | tf_op jit(solution)/shard_map/pallas_call | solution.py:124
  88.2 13.4 %shard_map.89 = (bf16[1024,1024]{1,0:T(8,128)(2,1)}, bf16[1024,1024]{1,0:T(8,128)(2,1)}, bf16[2,1024,1024]{2,1,0:T(8,128)(2,1)}) custom-call(s32[1]{0:T(128)} %bitcast.flag, f32[2,1024,1024]{2,1,0:T(8,128)} %anchor.7, bf16[512,1024]{1,0:T(8,128)(2,1)} %get-tuple-element.56.slope, bf16[512,1024]{1,0:T(8,128)(2,1)} %get-tuple-element.57.hidden.refs_2_, ...), custom_call_target="tpu_custom_call" | custom-call | flops 1 | bytes 1 | tf_op jit(solution)/shard_map/pallas_call | solution.py:199
  101.6 7.1 %shard_map.91 = (bf16[512,1024]{1,0:T(8,128)(2,1)}, bf16[512,1024]{1,0:T(8,128)(2,1)}, bf16[128,1024]{1,0:T(8,128)(2,1)}, bf16[128,1024]{1,0:T(8,128)(2,1)}, bf1...) custom-call(s32[1]{0:T(128)} %bitcast.flag, bf16[512,1024]{1,0:T(8,128)(2,1)} %shard_map.90.refs_0_.refs_3_, ...), custom_call_target="tpu_custom_call" | custom-call | flops 1 | bytes 1 | tf_op jit(solution)/shard_map/pallas_call | solution.py:124
  133.7 14.4 %shard_map.94 = (f32[2,1024,1024]{2,1,0:T(8,128)}, bf16[2,1024,1024]{2,1,0:T(8,128)(2,1)}, bf16[2,1024,1024]{2,1,0:T(8,128)(2,1)}) custom-call(s32[1]{0:T(128)} %bitcast.flag, bf16[2,1024,1024]{2,1,0:T(8,128)(2,1)} %get-tuple-element.59.refs_1_.weights, bf16[512,1024]{1,0:T(8,128)(2,1)} %get-tuple-element.60.slope, ...), custom_call_target="tpu_custom_call" | custom-call | flops 1 | bytes 1 | tf_op jit(solution)/shard_map/pallas_call | solution.py:199
  150.2 5.7 %collective-permute-start.26 = (bf16[2,1024,1024]{2,1,0:T(8,128)(2,1)}, bf16[2,1024,1024]{2,1,0:T(8,128)(2,1)}, u32[]{:S(2)}, u32[]{:S(2)}) collective-permute-start(bf16[2,1024,1024]{2,1,0:T(8,128)(2,1)} %shard_map.95.refs_1_.refs_2_), channel_id=1, source_target_pairs={{24,0},{0,8},{8,16},{16,24},{25,1},{1,9},{9,17},{17,25},{26,2},{2,... | collective-permute-start | bytes 12582920 | tf_op jit(solution)/shard_map/ppermute | solution.py:372
  155.9 6.2 %collective-permute-start.22 = (bf16[1024,1024]{1,0:T(8,128)(2,1)}, bf16[1024,1024]{1,0:T(8,128)(2,1)}, u32[]{:S(2)}, u32[]{:S(2)}) collective-permute-start(bf16[1024,1024]{1,0:T(8,128)(2,1)} %shard_map.96), channel_id=1, source_target_pairs={{0,4},{8,12},{16,20},{24,28},{1,5},{9,13},{17,21},{25,29},{2,6},{1... | collective-permute-start | bytes 6291464 | tf_op jit(solution)/shard_map/ppermute | solution.py:372
  173.9 11.2 %shard_map.100 = (bf16[512,1024]{1,0:T(8,128)(2,1)}, bf16[512,1024]{1,0:T(8,128)(2,1)}, bf16[2,1024,1024]{2,1,0:T(8,128)(2,1)}) custom-call(s32[1]{0:T(128)} %bitcast.flag, bf16[512,1024]{1,0:T(8,128)(2,1)} %copy-done.4, f32[2,1024,1024]{2,1,0:T(8,128)} %anchor.7, bf16[1024,1024]{1,0:T(8,128)(2,1)} %collective-permute-done.22.refs_2_.refs_0_, ...), custom_call_target="tpu_custom_call" | custom-call | flops 1 | bytes 1 | tf_op jit(solution)/shard_map/pallas_call | solution.py:124
  185.1 10.0 %shard_map.101.refs_1_ = bf16[2,1024,1024]{2,1,0:T(8,128)(2,1)} custom-call(s32[1]{0:T(128)} %bitcast.flag, bf16[2,1024,1024]{2,1,0:T(8,128)(2,1)} %get-tuple-element.70.weights.refs_2_, bf16[512,1024]{1,0:T(8,128)(2,1)} %get-tuple-element.71.slope, bf16[512,1024]{1,0:T(8,128)(2,1)} %get-tuple-element.72.hidden, ...), custom_call_target="tpu_custom_call" | custom-call | flops 1 | bytes 1 | tf_op jit(solution)/shard_map/pallas_call | solution.py:199
  195.1 10.2 %collective-permute-done.26.refs_3_ = bf16[2,1024,1024]{2,1,0:T(8,128)(2,1)} collective-permute-done((bf16[2,1024,1024]{2,1,0:T(8,128)(2,1)}, bf16[2,1024,1024]{2,1,0:T(8,128)(2,1)}, u32[]{:S(2)}, u32[]{:S(2)}) %collective-permute-start.26) | collective-permute-done | bytes 4194336 | tf_op jit(solution)/shard_map/ppermute | solution.py:372
  205.3 10.8 %shard_map.102 = (bf16[512,1024]{1,0:T(8,128)(2,1)}, bf16[512,1024]{1,0:T(8,128)(2,1)}, bf16[128,1024]{1,0:T(8,128)(2,1)}, bf16[128,1024]{1,0:T(8,128)(2,1)}, bf...) custom-call(s32[1]{0:T(128)} %bitcast.flag, bf16[512,1024]{1,0:T(8,128)(2,1)} %gather_fusion.1, ...), custom_call_target="tpu_custom_call" | custom-call | flops 1 | bytes 1 | tf_op jit(solution)/shard_map/pallas_call | solution.py:124
  220.6 5.0 %collective-permute-done.27 = bf16[128,1024]{1,0:T(8,128)(2,1)S(1)} collective-permute-done((bf16[128,1024]{1,0:T(8,128)(2,1)}, bf16[128,1024]{1,0:T(8,128)(2,1)S(1)}, u32[]{:S(2)}, u32[]{:S(2)}) %collective-permute-start.27) | collective-permute-done | bytes 262176 | tf_op jit(solution)/shard_map/ppermute | solution.py:23
  242.5 13.6 %shard_map.103 = (f32[2,1024,1024]{2,1,0:T(8,128)}, bf16[1024,1024]{1,0:T(8,128)(2,1)}, bf16[1024,1024]{1,0:T(8,128)(2,1)}) custom-call(s32[1]{0:T(128)} %bitcast.flag, bf16[2,1024,1024]{2,1,0:T(8,128)(2,1)} %get-tuple-element.73.weights, bf16[512,1024]{1,0:T(8,128)(2,1)} %get-tuple-element.74.slope, bf16[512,1024]{1,0:T(8,128)(2,1)} %get-tuple-element.75.hidden, ...), custom_call_target="tpu_custom_call" | custom-call | flops 1 | bytes 1 | tf_op jit(solution)/shard_map/pallas_call | solution.py:199
  266.6 10.8 %collective-permute-done.35 = bf16[256,1024]{1,0:T(8,128)(2,1)S(1)} collective-permute-done((bf16[256,1024]{1,0:T(8,128)(2,1)S(1)}, bf16[256,1024]{1,0:T(8,128)(2,1)S(1)}, u32[]{:S(2)}, u32[]{:S(2)}) %collective-permute-start.35) | collective-permute-done | bytes 524320 | tf_op jit(solution)/shard_map/ppermute | solution.py:307
  278.4 8.7 %collective-permute-start.41 = (bf16[256,1024]{1,0:T(8,128)(2,1)S(1)}, bf16[256,1024]{1,0:T(8,128)(2,1)}, u32[]{:S(2)}, u32[]{:S(2)}) collective-permute-start(bf16[256,1024]{1,0:T(8,128)(2,1)S(1)} %get-tuple-element.100), channel_id=1, source_target_pairs={{0,8},{4,12},{24,16},{28,20},{1,9},{5,13},{25,17},{29,21},{2,10},{... | collective-permute-start | bytes 1572872 | tf_op jit(solution)/shard_map/ppermute | solution.py:307
  290.6 8.0 %collective-permute-start.37 = (bf16[256,1024]{1,0:T(8,128)(2,1)}, bf16[256,1024]{1,0:T(8,128)(2,1)S(1)}, u32[]{:S(2)}, u32[]{:S(2)}) collective-permute-start(bf16[256,1024]{1,0:T(8,128)(2,1)} %shard_map.104), channel_id=1, source_target_pairs={{0,8},{4,12},{24,16},{28,20},{1,9},{5,13},{25,17},{29,21},{2,10},{... | collective-permute-start | bytes 1572872 | tf_op jit(solution)/shard_map/ppermute | solution.py:307
  304.7 6.1 %collective-permute-done.37 = bf16[256,1024]{1,0:T(8,128)(2,1)S(1)} collective-permute-done((bf16[256,1024]{1,0:T(8,128)(2,1)}, bf16[256,1024]{1,0:T(8,128)(2,1)S(1)}, u32[]{:S(2)}, u32[]{:S(2)}) %collective-permute-start.37) | collective-permute-done | bytes 524320 | tf_op jit(solution)/shard_map/ppermute | solution.py:307
  311.7 10.4 %collective-permute-done.47 = bf16[256,1024]{1,0:T(8,128)(2,1)S(1)} collective-permute-done((bf16[256,1024]{1,0:T(8,128)(2,1)S(1)}, bf16[256,1024]{1,0:T(8,128)(2,1)S(1)}, u32[]{:S(2)}, u32[]{:S(2)}) %collective-permute-start.47) | collective-permute-done | bytes 524320 | tf_op jit(solution)/shard_map/ppermute | solution.py:307
  323.7 9.6 %collective-permute-done.46 = bf16[256,1024]{1,0:T(8,128)(2,1)S(1)} collective-permute-done((bf16[256,1024]{1,0:T(8,128)(2,1)S(1)}, bf16[256,1024]{1,0:T(8,128)(2,1)S(1)}, u32[]{:S(2)}, u32[]{:S(2)}) %collective-permute-start.46) | collective-permute-done | bytes 524320 | tf_op jit(solution)/shard_map/ppermute | solution.py:307
  347.8 7.7 %collective-permute-done.39 = bf16[256,1024]{1,0:T(8,128)(2,1)S(1)} collective-permute-done((bf16[256,1024]{1,0:T(8,128)(2,1)S(1)}, bf16[256,1024]{1,0:T(8,128)(2,1)S(1)}, u32[]{:S(2)}, u32[]{:S(2)}) %collective-permute-start.39) | collective-permute-done | bytes 524320 | tf_op jit(solution)/shard_map/ppermute | solution.py:307
  (203 shorter events, 152.0 us)
Async XLA Ops:
  12.2 75.9 %collective-permute-start.10 = (bf16[2,1024,1024]{2,1,0:T(8,128)(2,1)}, bf16[2,1024,1024]{2,1,0:T(8,128)(2,1)}, u32[]{:S(2)}, u32[]{:S(2)}) collective-permute-start(bf16[2,1024,1024]{2,1,0:T(8,128)(2,1)} %shard_map.85.refs_2_), channel_id=1, source_target_pairs={{28,0},{0,4},{4,8},{8,12},{12,16},{16,20},{20,24},{24,28},{29,1},{... | collective-permute-start | bytes 12582920 | tf_op jit(solution)/shard_map/ppermute | solution.py:372
  26.2 13.8 %collective-permute-start.5 = (bf16[128,1024]{1,0:T(8,128)(2,1)}, bf16[128,1024]{1,0:T(8,128)(2,1)S(1)}, u32[]{:S(2)}, u32[]{:S(2)}) collective-permute-start(bf16[128,1024]{1,0:T(8,128)(2,1)} %get-tuple-element.53), channel_id=1, source_target_pairs={{0,2},{1,3},{2,0},{3,1},{4,6},{5,7},{6,4},{7,5},{8,10},{9,11},{10,... | collective-permute-start | bytes 786440 | tf_op jit(solution)/shard_map/ppermute | solution.py:23
  55.2 22.0 %collective-permute-start.11 = (bf16[512,1024]{1,0:T(8,128)(2,1)S(1)}, bf16[512,1024]{1,0:T(8,128)(2,1)S(1)}, u32[]{:S(2)}, u32[]{:S(2)}) collective-permute-start(bf16[512,1024]{1,0:T(8,128)(2,1)S(1)} %pad_maximum_fusion.refs_1_), channel_id=1, source_target_pairs={{28,0},{0,4},{4,8},{8,12},{12,16},{16,20},{20,24},{24,28},{29,1},{... | collective-permute-start | bytes 3145736 | tf_op jit(solution)/shard_map/ppermute | solution.py:372
  55.3 14.1 %collective-permute-start.3 = (bf16[128,1024]{1,0:T(8,128)(2,1)S(1)}, bf16[128,1024]{1,0:T(8,128)(2,1)S(1)}, u32[]{:S(2)}, u32[]{:S(2)}) collective-permute-start(bf16[128,1024]{1,0:T(8,128)(2,1)S(1)} %copy-done.12), channel_id=1, source_target_pairs={{0,3},{1,2},{2,1},{3,0},{4,7},{5,6},{6,5},{7,4},{8,11},{9,10},{10,... | collective-permute-start | bytes 786440 | tf_op jit(solution)/shard_map/ppermute | solution.py:23
  56.8 14.2 %collective-permute-start.2 = (bf16[128,1024]{1,0:T(8,128)(2,1)S(1)}, bf16[128,1024]{1,0:T(8,128)(2,1)S(1)}, u32[]{:S(2)}, u32[]{:S(2)}) collective-permute-start(bf16[128,1024]{1,0:T(8,128)(2,1)S(1)} %copy-done.12), channel_id=1, source_target_pairs={{0,2},{1,3},{2,0},{3,1},{4,6},{5,7},{6,4},{7,5},{8,10},{9,11},{10,... | collective-permute-start | bytes 786440 | tf_op jit(solution)/shard_map/ppermute | solution.py:23
  57.6 13.4 %collective-permute-start.1 = (bf16[128,1024]{1,0:T(8,128)(2,1)S(1)}, bf16[128,1024]{1,0:T(8,128)(2,1)S(1)}, u32[]{:S(2)}, u32[]{:S(2)}) collective-permute-start(bf16[128,1024]{1,0:T(8,128)(2,1)S(1)} %copy-done.12), channel_id=1, source_target_pairs={{0,1},{1,0},{2,3},{3,2},{4,5},{5,4},{6,7},{7,6},{8,9},{9,8},{10,11... | collective-permute-start | bytes 786440 | tf_op jit(solution)/shard_map/ppermute | solution.py:23
  78.2 55.3 %collective-permute-start.19 = (bf16[1024,1024]{1,0:T(8,128)(2,1)}, bf16[1024,1024]{1,0:T(8,128)(2,1)}, u32[]{:S(2)}, u32[]{:S(2)}) collective-permute-start(bf16[1024,1024]{1,0:T(8,128)(2,1)} %shard_map.92), channel_id=1, source_target_pairs={{24,0},{0,8},{8,16},{16,24},{25,1},{1,9},{9,17},{17,25},{26,2},{2,... | collective-permute-start | bytes 6291464 | tf_op jit(solution)/shard_map/ppermute | solution.py:372
  81.7 51.8 %collective-permute-start.20 = (bf16[1024,1024]{1,0:T(8,128)(2,1)}, bf16[1024,1024]{1,0:T(8,128)(2,1)}, u32[]{:S(2)}, u32[]{:S(2)}) collective-permute-start(bf16[1024,1024]{1,0:T(8,128)(2,1)} %shard_map.93), channel_id=1, source_target_pairs={{24,0},{0,8},{8,16},{16,24},{25,1},{1,9},{9,17},{17,25},{26,2},{2,... | collective-permute-start | bytes 6291464 | tf_op jit(solution)/shard_map/ppermute | solution.py:372
  129.9 18.3 %collective-permute-start.12 = (bf16[512,1024]{1,0:T(8,128)(2,1)S(1)}, bf16[512,1024]{1,0:T(8,128)(2,1)S(1)}, u32[]{:S(2)}, u32[]{:S(2)}) collective-permute-start(bf16[512,1024]{1,0:T(8,128)(2,1)S(1)} %copy-done.3), channel_id=1, source_target_pairs={{28,4},{4,12},{12,20},{20,28},{29,5},{5,13},{13,21},{21,29},{30,6}... | collective-permute-start | bytes 3145736 | tf_op jit(solution)/shard_map/ppermute | solution.py:372
  132.7 16.5 %collective-permute-start.21 = (bf16[512,1024]{1,0:T(8,128)(2,1)S(1)}, bf16[512,1024]{1,0:T(8,128)(2,1)S(1)}, u32[]{:S(2)}, u32[]{:S(2)}) collective-permute-start(bf16[512,1024]{1,0:T(8,128)(2,1)S(1)} %pad_maximum_fusion.1.refs_2_), channel_id=1, source_target_pairs={{28,4},{4,12},{12,20},{20,28},{29,5},{5,13},{13,21},{21,29},{30,6}... | collective-permute-start | bytes 3145736 | tf_op jit(solution)/shard_map/ppermute | solution.py:372
  150.2 55.1 %collective-permute-start.26 = (bf16[2,1024,1024]{2,1,0:T(8,128)(2,1)}, bf16[2,1024,1024]{2,1,0:T(8,128)(2,1)}, u32[]{:S(2)}, u32[]{:S(2)}) collective-permute-start(bf16[2,1024,1024]{2,1,0:T(8,128)(2,1)} %shard_map.95.refs_1_.refs_2_), channel_id=1, source_target_pairs={{24,0},{0,8},{8,16},{16,24},{25,1},{1,9},{9,17},{17,25},{26,2},{2,... | collective-permute-start | bytes 12582920 | tf_op jit(solution)/shard_map/ppermute | solution.py:372
  155.9 17.2 %collective-permute-start.22 = (bf16[1024,1024]{1,0:T(8,128)(2,1)}, bf16[1024,1024]{1,0:T(8,128)(2,1)}, u32[]{:S(2)}, u32[]{:S(2)}) collective-permute-start(bf16[1024,1024]{1,0:T(8,128)(2,1)} %shard_map.96), channel_id=1, source_target_pairs={{0,4},{8,12},{16,20},{24,28},{1,5},{9,13},{17,21},{25,29},{2,6},{1... | collective-permute-start | bytes 6291464 | tf_op jit(solution)/shard_map/ppermute | solution.py:372
  218.3 13.0 %collective-permute-start.29 = (bf16[128,1024]{1,0:T(8,128)(2,1)}, bf16[128,1024]{1,0:T(8,128)(2,1)S(1)}, u32[]{:S(2)}, u32[]{:S(2)}) collective-permute-start(bf16[128,1024]{1,0:T(8,128)(2,1)} %get-tuple-element.81), channel_id=1, source_target_pairs={{0,3},{1,2},{2,1},{3,0},{4,7},{5,6},{6,5},{7,4},{8,11},{9,10},{10,... | collective-permute-start | bytes 786440 | tf_op jit(solution)/shard_map/ppermute | solution.py:23
  263.9 13.5 %collective-permute-start.35 = (bf16[256,1024]{1,0:T(8,128)(2,1)S(1)}, bf16[256,1024]{1,0:T(8,128)(2,1)S(1)}, u32[]{:S(2)}, u32[]{:S(2)}) collective-permute-start(bf16[256,1024]{1,0:T(8,128)(2,1)S(1)} %get-tuple-element.96), channel_id=1, source_target_pairs={{0,8},{4,12},{24,16},{28,20},{1,9},{5,13},{25,17},{29,21},{2,10},{... | collective-permute-start | bytes 1572872 | tf_op jit(solution)/shard_map/ppermute | solution.py:307
  265.3 23.4 %collective-permute-start.44 = (bf16[256,1024]{1,0:T(8,128)(2,1)S(1)}, bf16[256,1024]{1,0:T(8,128)(2,1)S(1)}, u32[]{:S(2)}, u32[]{:S(2)}) collective-permute-start(bf16[256,1024]{1,0:T(8,128)(2,1)S(1)} %get-tuple-element.95), channel_id=1, source_target_pairs={{0,8},{4,12},{24,16},{28,20},{1,9},{5,13},{25,17},{29,21},{2,10},{... | collective-permute-start | bytes 1572872 | tf_op jit(solution)/shard_map/ppermute | solution.py:307
  278.4 21.6 %collective-permute-start.41 = (bf16[256,1024]{1,0:T(8,128)(2,1)S(1)}, bf16[256,1024]{1,0:T(8,128)(2,1)}, u32[]{:S(2)}, u32[]{:S(2)}) collective-permute-start(bf16[256,1024]{1,0:T(8,128)(2,1)S(1)} %get-tuple-element.100), channel_id=1, source_target_pairs={{0,8},{4,12},{24,16},{28,20},{1,9},{5,13},{25,17},{29,21},{2,10},{... | collective-permute-start | bytes 1572872 | tf_op jit(solution)/shard_map/ppermute | solution.py:307
  288.9 14.3 %collective-permute-start.45 = (bf16[256,1024]{1,0:T(8,128)(2,1)S(1)}, bf16[256,1024]{1,0:T(8,128)(2,1)S(1)}, u32[]{:S(2)}, u32[]{:S(2)}) collective-permute-start(bf16[256,1024]{1,0:T(8,128)(2,1)S(1)} %fusion.6), channel_id=1, source_target_pairs={{8,16},{12,20},{16,8},{20,12},{9,17},{13,21},{17,9},{21,13},{10,18... | collective-permute-start | bytes 1572872 | tf_op jit(solution)/shard_map/ppermute | solution.py:307
  290.6 20.2 %collective-permute-start.37 = (bf16[256,1024]{1,0:T(8,128)(2,1)}, bf16[256,1024]{1,0:T(8,128)(2,1)S(1)}, u32[]{:S(2)}, u32[]{:S(2)}) collective-permute-start(bf16[256,1024]{1,0:T(8,128)(2,1)} %shard_map.104), channel_id=1, source_target_pairs={{0,8},{4,12},{24,16},{28,20},{1,9},{5,13},{25,17},{29,21},{2,10},{... | collective-permute-start | bytes 1572872 | tf_op jit(solution)/shard_map/ppermute | solution.py:307
  301.2 21.0 %collective-permute-start.42 = (bf16[256,1024]{1,0:T(8,128)(2,1)S(1)}, bf16[256,1024]{1,0:T(8,128)(2,1)S(1)}, u32[]{:S(2)}, u32[]{:S(2)}) collective-permute-start(bf16[256,1024]{1,0:T(8,128)(2,1)S(1)} %fusion.4), channel_id=1, source_target_pairs={{8,16},{12,20},{16,8},{20,12},{9,17},{13,21},{17,9},{21,13},{10,18... | collective-permute-start | bytes 1572872 | tf_op jit(solution)/shard_map/ppermute | solution.py:307
  301.9 20.2 %collective-permute-start.47 = (bf16[256,1024]{1,0:T(8,128)(2,1)S(1)}, bf16[256,1024]{1,0:T(8,128)(2,1)S(1)}, u32[]{:S(2)}, u32[]{:S(2)}) collective-permute-start(bf16[256,1024]{1,0:T(8,128)(2,1)S(1)} %copy-done.7), channel_id=1, source_target_pairs={{8,0},{12,4},{16,24},{20,28},{9,1},{13,5},{17,25},{21,29},{10,2},{... | collective-permute-start | bytes 1572872 | tf_op jit(solution)/shard_map/ppermute | solution.py:307
  303.4 29.9 %collective-permute-start.46 = (bf16[256,1024]{1,0:T(8,128)(2,1)S(1)}, bf16[256,1024]{1,0:T(8,128)(2,1)S(1)}, u32[]{:S(2)}, u32[]{:S(2)}) collective-permute-start(bf16[256,1024]{1,0:T(8,128)(2,1)S(1)} %fusion.7), channel_id=1, source_target_pairs={{8,0},{12,4},{16,24},{20,28},{9,1},{13,5},{17,25},{21,29},{10,2},{... | collective-permute-start | bytes 1572872 | tf_op jit(solution)/shard_map/ppermute | solution.py:307
  311.0 28.1 %collective-permute-start.38 = (bf16[256,1024]{1,0:T(8,128)(2,1)S(1)}, bf16[256,1024]{1,0:T(8,128)(2,1)S(1)}, u32[]{:S(2)}, u32[]{:S(2)}) collective-permute-start(bf16[256,1024]{1,0:T(8,128)(2,1)S(1)} %fusion.2), channel_id=1, source_target_pairs={{8,16},{12,20},{16,8},{20,12},{9,17},{13,21},{17,9},{21,13},{10,18... | collective-permute-start | bytes 1572872 | tf_op jit(solution)/shard_map/ppermute | solution.py:307
  322.4 19.6 %collective-permute-start.43 = (bf16[256,1024]{1,0:T(8,128)(2,1)S(1)}, bf16[256,1024]{1,0:T(8,128)(2,1)S(1)}, u32[]{:S(2)}, u32[]{:S(2)}) collective-permute-start(bf16[256,1024]{1,0:T(8,128)(2,1)S(1)} %fusion.5), channel_id=1, source_target_pairs={{8,0},{12,4},{16,24},{20,28},{9,1},{13,5},{17,25},{21,29},{10,2},{... | collective-permute-start | bytes 1572872 | tf_op jit(solution)/shard_map/ppermute | solution.py:307
  339.3 16.2 %collective-permute-start.39 = (bf16[256,1024]{1,0:T(8,128)(2,1)S(1)}, bf16[256,1024]{1,0:T(8,128)(2,1)S(1)}, u32[]{:S(2)}, u32[]{:S(2)}) collective-permute-start(bf16[256,1024]{1,0:T(8,128)(2,1)S(1)} %fusion.3), channel_id=1, source_target_pairs={{8,0},{12,4},{16,24},{20,28},{9,1},{13,5},{17,25},{21,29},{10,2},{... | collective-permute-start | bytes 1572872 | tf_op jit(solution)/shard_map/ppermute | solution.py:307
  (57 other events, 419.3 us)
where the time goes:
time: 373 us; the launch traced here: 366 us
  Pallas kernels  122 us (33%)
  waiting for transfers between devices  119 us (32%)
  starting transfers between devices  82.7 us (22%)
  local copies, waits for them, and re-layouts  24.7 us (7%)
  other arithmetic  16.2 us (4%)
    pallas_call x5, Pallas kernels, backward(): pl.pallas_call(functools.partial(backward_kernel, update, counts, (len(er...  62 us
    ppermute x27, waiting for transfers between devices, swapped(): lax.ppermute(block, axis, [(i, i ^ mask) for i in range(lax.axis_size(axi...  56.9 us
    ppermute x12, waiting for transfers between devices, moved(): lax.ppermute(part, axis, [(cores * a + c, cores * b + c) for a, b in hops...  48.9 us
    pallas_call x5, Pallas kernels, forward(): pl.pallas_call(functools.partial(forward_kernel, mix, counts, len(inputs)...  43.4 us
    ppermute x12, starting transfers between devices, sent(): return lax.ppermute(block, 'replica', route)  29.9 us
    ppermute x12, starting transfers between devices, moved(): lax.ppermute(part, axis, [(cores * a + c, cores * b + c) for a, b in hops...  27.2 us
    ppermute x27, starting transfers between devices, swapped(): lax.ppermute(block, axis, [(i, i ^ mask) for i in range(lax.axis_size(axi...  25.6 us
    pallas_call x4, Pallas kernels, finish(): pl.pallas_call(functools.partial(finish_kernel, replicas), grid=(steps,),...  16.5 us
  transfers between devices with their start and end apart: 51, of which 28 were waited for; matrix products, arithmetic and copies ran while one was open for 7% of the time, Pallas kernels for 25%

commit v1 on v0

--- a/solution.py
+++ b/solution.py
@@ -171,11 +171,17 @@
                 result[k] = value.astype(result.dtype)
                 continue
             if apart:
-                for place, piece in enumerate(result):
-
-                    @pl.when((flag[0] == k) == (place == 0))
-                    def _():
-                        piece[...] = value.astype(piece.dtype)
+                mine, *others = result
+
+                @pl.when(flag[0] == k)
+                def _():
+                    mine[...] = value.astype(mine.dtype)
+
+                @pl.when(flag[0] != k)
+                def _():
+                    size = others[0].shape[0]
+                    for i, piece in enumerate(others):
+                        piece[...] = value[i * size : (i + 1) * size].astype(piece.dtype)
 
                 continue
             each = len(result) // 2
@@ -191,11 +197,14 @@
     counts, flat = flattened(states)
     kinds = [kind if type(kind) is tuple else (kind, 1) for kind in kinds]
     by_core = [count == "core" for _, count in kinds]
-    kinds = [(kind, 2 if apart else count) for (kind, count), apart in zip(kinds, by_core)]
+    kinds = [(kind, 3 if apart else count) for (kind, count), apart in zip(kinds, by_core)]
     shapes = []
-    for kind, count in kinds:
-        shape = weights.shape if count == 1 else (2 * width // count, units)
-        shapes += [jax.ShapeDtypeStruct(shape, kind)] * count
+    for (kind, count), apart in zip(kinds, by_core):
+        if apart:
+            parts = [(width, units), (width // 2, units), (width // 2, units)]
+        else:
+            parts = [weights.shape if count == 1 else (2 * width // count, units)] * count
+        shapes += [jax.ShapeDtypeStruct(part, kind) for part in parts]
     results = pl.pallas_call(
         functools.partial(
             backward_kernel, update, counts, (len(errors), len(inputs)), [count for _, count in kinds], by_core
@@ -293,7 +302,7 @@
     )(flag, slow, anchor, own, theirs, *before)
 
 
-def slow_step(flag, mine, other, slow, anchor):
+def slow_step(flag, mine, others, slow, anchor):
     axis, cores = "replica", 2
     index = lax.axis_index(axis)
     replicas = lax.axis_size(axis)
@@ -315,13 +324,12 @@
     stages += [(False, [(s + 1, s), (length - 2 - s, length - 1 - s)]) for s in reversed(range(half - 1))]
 
     pair_rows = rows // 2
-    pairs = [swapped(other[p * pair_rows : (p + 1) * pair_rows], axis, 1) for p in range(2)]
+    pairs = [swapped(part, axis, 1) for part in others]
     blocks = []
     for c in range(chunks):
         p, start = divmod(c * size, pair_rows)
         blocks.append(added(mine[c * size : (c + 1) * size], pairs[p][start : start + size]))
-    arrived, made, results, tokens = {}, {}, [], []
-    final = len(stages) - 1
+    arrived, results, tokens = {}, [], []
     for tick in range(chunks + len(stages)):
         for s in reversed(range(len(stages) + 1)):
             c = tick - s
@@ -332,11 +340,11 @@
                 adds, hops = stages[s - 1]
                 fresh = added(block, arrived[s - 1, c]) if adds else arrived[s - 1, c]
                 block = jnp.where(at([b for _, b in hops]), fresh, block)
-                if s > final and 0 < c < chunks - 1:
+                if s == len(stages) and c:
                     block = tied([tokens[c - 1]], block)
-            if s == 0 and c >= 3 and (2, c - 3) in made:
-                block = tied([made[2, c - 3]], block)
-            blocks[c] = made[s, c] = block
+                if s == 1 and c:
+                    block = tied([blocks[c - 1]], block)
+            blocks[c] = block
             if s < len(stages):
                 arrived[s, c] = moved(block, stages[s][1])
             else:
@@ -374,8 +382,10 @@
     def picked(step, count):
         return tokens.at[picks_all[step, :count]].get(mode="promise_in_bounds")
 
-    near_share = sent(picked(0, share_rows), 1)
-    narrow = tied([near_share], momentum[0].astype(bf16))
+    shares = jnp.concatenate([picks_all[step, :share_rows] for step in range(2)])
+    shares = sent(tokens.at[shares].get(mode="promise_in_bounds"), 1)
+    near_share, far_share = shares[:share_rows], shares[share_rows:]
+    narrow = tied([shares], momentum[0].astype(bf16))
     moment_near = sent(narrow, 1)
 
     inputs = [picked(0, row_count)]
@@ -391,11 +401,11 @@
         inputs,
         [momentum[0]],
         first_update,
-        [f32, (bf16, 2)],
+        [f32, bf16],
     )
     inputs_near = gathered(near_share)
     hidden_near, slope_near = forward(flag, inputs_near, [anchor], only, 0, emits=False, waits=[moment])
-    moment_far = [sent(tied([error_near, hidden_near], part), 2, (0,)) for part in moment_bf]
+    moment_far = sent(tied([error_near, hidden_near], moment_bf), 2, (0,))
     moment_near, weights = backward(
         flag,
         [error_near],
@@ -408,8 +418,7 @@
         [(bf16, 2), bf16],
     )
 
-    inputs = [tied([moment_near[0]], picked(1, row_count))]
-    inputs_far = sent(inputs[0], 2, (1,))
+    inputs = [picked(1, row_count)]
     hidden, slope, *partials = forward(flag, inputs, [weights], only, tensors, emits=False)
     error = jnp.concatenate(gathered(error_share(partials, 1)))
     error_far = sent(error, 2, (1,))
@@ -423,15 +432,16 @@
         [moment, weights],
         second_update,
         [f32, bf16, bf16],
-        waits=moment_far,
-    )
-    weights = tied([error_far, inputs_far], weights)
+        waits=[moment_far],
+    )
+    weights = tied([error_far], weights)
     weights_sent = sent(weights, 2, (0,))
+    inputs_far = gathered(sent(tied([weights], far_share), 1, (1,)))
     moment_two = tuple(sent(tied([weights], part), 1, (1,)) for part in moment_near)
-    moment_three = tuple(sent(tied([weights], part), 1, (1,)) for part in moment_far)
-    hidden, slope, weights_far = forward(flag, [inputs_far], [anchor, moment_two, moment_three], pushed, 0)
+    moment_three = tuple(sent(tied([weights], moment_far[k]), 1, (1,)) for k in range(2))
+    hidden, slope, weights_far = forward(flag, inputs_far, [anchor, moment_two, moment_three], pushed, 0)
     (weights_found,) = backward(
-        flag, [error_far], weights_far, slope, hidden, [inputs_far], [moment_two, weights_far], second_beside, [bf16]
+        flag, [error_far], weights_far, slope, hidden, inputs_far, [moment_two, weights_far], second_beside, [bf16]
     )
 
     inputs = [picked(2, row_count)]
@@ -440,7 +450,7 @@
     moment, total = backward(
         flag, errors, rest[tensors], slope, hidden, inputs, [moment, known], third_update, [f32, (bf16, "core")]
     )
-    anchor_new, slow_new = slow_step(flag, *total, slow, anchor)
+    anchor_new, slow_new = slow_step(flag, total[0], total[1:], slow, anchor)
     return (anchor_new, slow_new, moment[None])
 
 

time: 373 us -> 391 us (1.048)
  waiting for transfers between devices: 119 us -> 129 us
  other arithmetic: 16.2 us -> 24.9 us
    ppermute x27 -> x30, waiting for transfers between devices: 56.9 us -> 73.4 us  [swapped(): lax.ppermute(block, axis, [(i, i ^ mask) for i in range(lax.axis_size(axi...]
    ppermute x12 -> x11, waiting for transfers between devices: 13.1 us -> 4.56 us  [sent(): return lax.ppermute(block, 'replica', route)]
    select_n x12, other arithmetic: 5.24 us -> 12.6 us  [slow_step(): block = jnp.where(at([b for _, b in hops]), fresh, block)]
    ppermute x12 -> x11, starting transfers between devices: 29.9 us -> 23.2 us  [sent(): return lax.ppermute(block, 'replica', route)]
    squeeze x0 -> x1, local copies, waits for them, and re-layouts: none -> 4.68 us  [body(): moment_far[k]]
    ppermute x27 -> x30, starting transfers between devices: 25.6 us -> 29.4 us  [swapped(): lax.ppermute(block, axis, [(i, i ^ mask) for i in range(lax.axis_size(axi...]
    unnamed x60 -> x56, local copies, waits for them, and re-layouts: 9.64 us -> 7.94 us
    gather x4 -> x3, local copies, waits for them, and re-layouts: 9.28 us -> 8.38 us  [picked(): return tokens.at[picks_all[step, :count]].get(mode='promise_in_bounds')]
  transfers between devices with their start and end apart: 51 -> 53, of which waited for: 28 -> 27; matrix products, arithmetic and copies ran while one was open for 7% -> 10% of each run, Pallas kernels for 25% -> 23%
where the time goes in v1:
time: 391 us; the launch traced here: 384 us
  waiting for transfers between devices  129 us (33%)
  Pallas kernels  121 us (31%)
  starting transfers between devices  79.6 us (20%)
  local copies, waits for them, and re-layouts  28.2 us (7%)
  other arithmetic  24.9 us (6%)
    ppermute x30, waiting for transfers between devices, swapped(): lax.ppermute(block, axis, [(i, i ^ mask) for i in range(lax.axis_size(axi...  73.4 us
    pallas_call x5, Pallas kernels, backward(): pl.pallas_call(functools.partial(backward_kernel, update, counts, (len(er...  62.4 us
    ppermute x12, waiting for transfers between devices, moved(): lax.ppermute(part, axis, [(cores * a + c, cores * b + c) for a, b in hops...  50.7 us
    pallas_call x5, Pallas kernels, forward(): pl.pallas_call(functools.partial(forward_kernel, mix, counts, len(inputs)...  42.1 us
    ppermute x30, starting transfers between devices, swapped(): lax.ppermute(block, axis, [(i, i ^ mask) for i in range(lax.axis_size(axi...  29.4 us
    ppermute x12, starting transfers between devices, moved(): lax.ppermute(part, axis, [(cores * a + c, cores * b + c) for a, b in hops...  27 us
    ppermute x11, starting transfers between devices, sent(): return lax.ppermute(block, 'replica', route)  23.2 us
    pallas_call x4, Pallas kernels, finish(): pl.pallas_call(functools.partial(finish_kernel, replicas), grid=(steps,),...  16.5 us
  transfers between devices with their start and end apart: 53, of which 27 were waited for; matrix products, arithmetic and copies ran while one was open for 10% of the time, Pallas kernels for 23%

profile of v1, /device:TPU:0, one launch (start us, length us, event | category | flops | bytes accessed | tf_op | source)
XLA Modules:
  0.0 384.0 jit_solution(18140474854660353380)
XLA Ops:
  6.5 6.1 %bitcast_convert_fusion.refs_0_ = bf16[2,1024,1024]{2,1,0:T(8,128)(2,1)} fusion(f32[1,2,1024,1024]{3,2,1,0:T(8,128)} %param.10), kind=kLoop, calls=%fused_computation.65 | loop fusion | flops 2097152 | bytes 12582912 | tf_op jit(solution)/shard_map/convert_element_type | solution.py:388
  16.1 8.9 %shard_map.86 = (bf16[512,1024]{1,0:T(8,128)(2,1)}, bf16[512,1024]{1,0:T(8,128)(2,1)}, bf16[128,1024]{1,0:T(8,128)(2,1)}, bf16[128,1024]{1,0:T(8,128)(2,1)}, bf1...) custom-call(s32[1]{0:T(128)} %bitcast.flag, bf16[512,1024]{1,0:T(8,128)(2,1)} %gather_fusion.3, ...), custom_call_target="tpu_custom_call" | custom-call | flops 1 | bytes 1 | tf_op jit(solution)/shard_map/pallas_call | solution.py:124
  29.5 5.9 %collective-permute-done.6 = bf16[128,1024]{1,0:T(8,128)(2,1)S(1)} collective-permute-done((bf16[128,1024]{1,0:T(8,128)(2,1)}, bf16[128,1024]{1,0:T(8,128)(2,1)S(1)}, u32[]{:S(2)}, u32[]{:S(2)}) %collective-permute-start.6) | collective-permute-done | bytes 262176 | tf_op jit(solution)/shard_map/ppermute | solution.py:23
  44.9 6.6 %collective-permute-done.9 = bf16[128,1024]{1,0:T(8,128)(2,1)S(1)} collective-permute-done((bf16[128,1024]{1,0:T(8,128)(2,1)S(1)}, bf16[128,1024]{1,0:T(8,128)(2,1)S(1)}, u32[]{:S(2)}, u32[]{:S(2)}) %collective-permute-start.9) | collective-permute-done | bytes 262176 | tf_op jit(solution)/shard_map/ppermute | solution.py:23
  62.0 10.9 %shard_map.87 = (f32[2,1024,1024]{2,1,0:T(8,128)}, bf16[2,1024,1024]{2,1,0:T(8,128)(2,1)}) custom-call(s32[1]{0:T(128)} %bitcast.flag, f32[2,1024,1024]{2,1,0:T(8,128)} %anchor.7, bf16[512,1024]{1,0:T(8,128)(2,1)} %get-tuple-element.50.slope, bf16[512,1024]{1,0:T(8,128)(2,1)} %get-tuple-element.51.hidden, f32[2,1024,1024]{2,1,0:T(8,128)} %bitcast.48, ...), custom_call_target="tpu_custom_call" | custom-call | flops 1 | bytes 1 | tf_op jit(solution)/shard_map/pallas_call | solution.py:208
  75.3 5.4 %shard_map.88 = (bf16[512,1024]{1,0:T(8,128)(2,1)}, bf16[512,1024]{1,0:T(8,128)(2,1)}) custom-call(s32[1]{0:T(128)} %bitcast.flag, bf16[128,1024]{1,0:T(8,128)(2,1)} %copy-done.10, bf16[128,1024]{1,0:T(8,128)(2,1)} %copy-done.17, bf16[128,1024]{1,0:T(8,128)(2,1)} %copy-done.18, bf16[128,1024]{1,0:T(8,128)(2,1)} %copy-done.19, f32[2,1024,1024]{2,1,0:T(8,128)} %anchor.7, ...), custom_call_target="tpu_custom_call" | custom-call | flops 1 | bytes 1 | tf_op jit(solution)/shard_map/pallas_call | solution.py:124
  88.2 13.5 %shard_map.89 = (bf16[1024,1024]{1,0:T(8,128)(2,1)}, bf16[1024,1024]{1,0:T(8,128)(2,1)}, bf16[2,1024,1024]{2,1,0:T(8,128)(2,1)}) custom-call(s32[1]{0:T(128)} %bitcast.flag, f32[2,1024,1024]{2,1,0:T(8,128)} %anchor.7, bf16[512,1024]{1,0:T(8,128)(2,1)} %get-tuple-element.57.slope, bf16[512,1024]{1,0:T(8,128)(2,1)} %get-tuple-element.58.hidden.refs_2_, ...), custom_call_target="tpu_custom_call" | custom-call | flops 1 | bytes 1 | tf_op jit(solution)/shard_map/pallas_call | solution.py:208
  101.7 7.0 %shard_map.90 = (bf16[512,1024]{1,0:T(8,128)(2,1)}, bf16[512,1024]{1,0:T(8,128)(2,1)}, bf16[128,1024]{1,0:T(8,128)(2,1)}, bf16[128,1024]{1,0:T(8,128)(2,1)}, bf1...) custom-call(s32[1]{0:T(128)} %bitcast.flag, bf16[512,1024]{1,0:T(8,128)(2,1)} %gather_fusion.5, ...), custom_call_target="tpu_custom_call" | custom-call | flops 1 | bytes 1 | tf_op jit(solution)/shard_map/pallas_call | solution.py:124
  113.1 6.0 %collective-permute-done.14 = bf16[128,1024]{1,0:T(8,128)(2,1)S(1)} collective-permute-done((bf16[128,1024]{1,0:T(8,128)(2,1)}, bf16[128,1024]{1,0:T(8,128)(2,1)S(1)}, u32[]{:S(2)}, u32[]{:S(2)}) %collective-permute-start.14) | collective-permute-done | bytes 262176 | tf_op jit(solution)/shard_map/ppermute | solution.py:23
  127.9 6.6 %collective-permute-done.17 = bf16[128,1024]{1,0:T(8,128)(2,1)S(1)} collective-permute-done((bf16[128,1024]{1,0:T(8,128)(2,1)S(1)}, bf16[128,1024]{1,0:T(8,128)(2,1)S(1)}, u32[]{:S(2)}, u32[]{:S(2)}) %collective-permute-start.17) | collective-permute-done | bytes 262176 | tf_op jit(solution)/shard_map/ppermute | solution.py:23
  140.4 14.3 %shard_map.92 = (f32[2,1024,1024]{2,1,0:T(8,128)}, bf16[2,1024,1024]{2,1,0:T(8,128)(2,1)}, bf16[2,1024,1024]{2,1,0:T(8,128)(2,1)}) custom-call(s32[1]{0:T(128)} %bitcast.flag, bf16[2,1024,1024]{2,1,0:T(8,128)(2,1)} %get-tuple-element.59.refs_1_.weights, bf16[512,1024]{1,0:T(8,128)(2,1)} %get-tuple-element.60.slope, ...), custom_call_target="tpu_custom_call" | custom-call | flops 1 | bytes 1 | tf_op jit(solution)/shard_map/pallas_call | solution.py:208
  186.8 10.1 %shard_map.99 = (bf16[512,1024]{1,0:T(8,128)(2,1)}, bf16[512,1024]{1,0:T(8,128)(2,1)}, bf16[2,1024,1024]{2,1,0:T(8,128)(2,1)}) custom-call(s32[1]{0:T(128)} %bitcast.flag, bf16[128,1024]{1,0:T(8,128)(2,1)} %copy-done.13, bf16[128,1024]{1,0:T(8,128)(2,1)} %copy-done.14, bf16[128,1024]{1,0:T(8,128)(2,1)} %copy-done.15, bf16[128,1024]{1,0:T(8,128)(2,1)} %copy-done.16, ...), custom_call_target="tpu_custom_call" | custom-call | flops 1 | bytes 1 | tf_op jit(solution)/shard_map/pallas_call | solution.py:124
  196.9 10.2 %shard_map.100.refs_1_ = bf16[2,1024,1024]{2,1,0:T(8,128)(2,1)} custom-call(s32[1]{0:T(128)} %bitcast.flag, bf16[2,1024,1024]{2,1,0:T(8,128)(2,1)} %get-tuple-element.70.weights.refs_2_, bf16[512,1024]{1,0:T(8,128)(2,1)} %get-tuple-element.71.slope, bf16[512,1024]{1,0:T(8,128)(2,1)} %get-tuple-element.72.hidden, ...), custom_call_target="tpu_custom_call" | custom-call | flops 1 | bytes 1 | tf_op jit(solution)/shard_map/pallas_call | solution.py:208
  208.2 10.8 %shard_map.101 = (bf16[512,1024]{1,0:T(8,128)(2,1)}, bf16[512,1024]{1,0:T(8,128)(2,1)}, bf16[128,1024]{1,0:T(8,128)(2,1)}, bf16[128,1024]{1,0:T(8,128)(2,1)}, bf...) custom-call(s32[1]{0:T(128)} %bitcast.flag, bf16[512,1024]{1,0:T(8,128)(2,1)} %gather_fusion.1, ...), custom_call_target="tpu_custom_call" | custom-call | flops 1 | bytes 1 | tf_op jit(solution)/shard_map/pallas_call | solution.py:124
  223.4 6.0 %collective-permute-done.31 = bf16[128,1024]{1,0:T(8,128)(2,1)S(1)} collective-permute-done((bf16[128,1024]{1,0:T(8,128)(2,1)}, bf16[128,1024]{1,0:T(8,128)(2,1)S(1)}, u32[]{:S(2)}, u32[]{:S(2)}) %collective-permute-start.31) | collective-permute-done | bytes 262176 | tf_op jit(solution)/shard_map/ppermute | solution.py:23
  238.0 5.7 %collective-permute-done.32.refs_3_ = bf16[128,1024]{1,0:T(8,128)(2,1)S(1)} collective-permute-done((bf16[128,1024]{1,0:T(8,128)(2,1)S(1)}, bf16[128,1024]{1,0:T(8,128)(2,1)S(1)}, u32[]{:S(2)}, u32[]{:S(2)}) %collective-permute-start.32) | collective-permute-done | bytes 262176 | tf_op jit(solution)/shard_map/ppermute | solution.py:23
  243.7 5.7 %collective-permute-done.33.refs_4_ = bf16[128,1024]{1,0:T(8,128)(2,1)S(1)} collective-permute-done((bf16[128,1024]{1,0:T(8,128)(2,1)S(1)}, bf16[128,1024]{1,0:T(8,128)(2,1)S(1)}, u32[]{:S(2)}, u32[]{:S(2)}) %collective-permute-start.33) | collective-permute-done | bytes 262176 | tf_op jit(solution)/shard_map/ppermute | solution.py:23
  250.1 13.6 %shard_map.102 = (f32[2,1024,1024]{2,1,0:T(8,128)}, bf16[1024,1024]{1,0:T(8,128)(2,1)}, bf16[512,1024]{1,0:T(8,128)(2,1)}, bf16[512,1024]{1,0:T(8,128)(2,1)}) custom-call(s32[1]{0:T(128)} %bitcast.flag, bf16[2,1024,1024]{2,1,0:T(8,128)(2,1)} %get-tuple-element.73.weights, bf16[512,1024]{1,0:T(8,128)(2,1)} %get-tuple-element.74.slope, ...), custom_call_target="tpu_custom_call" | custom-call | flops 1 | bytes 1 | tf_op jit(solution)/shard_map/pallas_call | solution.py:208
  275.5 10.9 %collective-permute-done.40 = bf16[256,1024]{1,0:T(8,128)(2,1)S(1)} collective-permute-done((bf16[256,1024]{1,0:T(8,128)(2,1)S(1)}, bf16[256,1024]{1,0:T(8,128)(2,1)S(1)}, u32[]{:S(2)}, u32[]{:S(2)}) %collective-permute-start.40) | collective-permute-done | bytes 524320 | tf_op jit(solution)/shard_map/ppermute | solution.py:316
  287.3 5.9 %collective-permute-start.37 = (bf16[256,1024]{1,0:T(8,128)(2,1)S(1)}, bf16[256,1024]{1,0:T(8,128)(2,1)S(1)}, u32[]{:S(2)}, u32[]{:S(2)}) collective-permute-start(bf16[256,1024]{1,0:T(8,128)(2,1)S(1)} %get-tuple-element.104), channel_id=1, source_target_pairs={{0,8},{4,12},{24,16},{28,20},{1,9},{5,13},{25,17},{29,21},{2,10},{... | collective-permute-start | bytes 1572872 | tf_op jit(solution)/shard_map/ppermute | solution.py:316
  300.4 8.1 %collective-permute-start.36 = (bf16[256,1024]{1,0:T(8,128)(2,1)S(1)}, bf16[256,1024]{1,0:T(8,128)(2,1)S(1)}, u32[]{:S(2)}, u32[]{:S(2)}) collective-permute-start(bf16[256,1024]{1,0:T(8,128)(2,1)S(1)} %get-tuple-element.103), channel_id=1, source_target_pairs={{0,8},{4,12},{24,16},{28,20},{1,9},{5,13},{25,17},{29,21},{2,10},{... | collective-permute-start | bytes 1572872 | tf_op jit(solution)/shard_map/ppermute | solution.py:316
  315.1 8.8 %collective-permute-done.48 = bf16[256,1024]{1,0:T(8,128)(2,1)} collective-permute-done((bf16[256,1024]{1,0:T(8,128)(2,1)}, bf16[256,1024]{1,0:T(8,128)(2,1)}, u32[]{:S(2)}, u32[]{:S(2)}) %collective-permute-start.48) | collective-permute-done | bytes 524320 | tf_op jit(solution)/shard_map/ppermute | solution.py:316
  343.2 16.4 %collective-permute-done.46 = bf16[256,1024]{1,0:T(8,128)(2,1)S(1)} collective-permute-done((bf16[256,1024]{1,0:T(8,128)(2,1)S(1)}, bf16[256,1024]{1,0:T(8,128)(2,1)S(1)}, u32[]{:S(2)}, u32[]{:S(2)}) %collective-permute-start.46) | collective-permute-done | bytes 524320 | tf_op jit(solution)/shard_map/ppermute | solution.py:316
  360.4 10.2 %collective-permute-done.45 = bf16[256,1024]{1,0:T(8,128)(2,1)S(1)} collective-permute-done((bf16[256,1024]{1,0:T(8,128)(2,1)S(1)}, bf16[256,1024]{1,0:T(8,128)(2,1)S(1)}, u32[]{:S(2)}, u32[]{:S(2)}) %collective-permute-start.45) | collective-permute-done | bytes 524320 | tf_op jit(solution)/shard_map/ppermute | solution.py:316
  (209 shorter events, 168.8 us)
Async XLA Ops:
  15.4 72.8 %collective-permute-start.10 = (bf16[2,1024,1024]{2,1,0:T(8,128)(2,1)}, bf16[2,1024,1024]{2,1,0:T(8,128)(2,1)}, u32[]{:S(2)}, u32[]{:S(2)}) collective-permute-start(bf16[2,1024,1024]{2,1,0:T(8,128)(2,1)} %shard_map.85.refs_2_), channel_id=1, source_target_pairs={{28,0},{0,4},{4,8},{8,12},{12,16},{16,20},{20,24},{24,28},{29,1},{... | collective-permute-start | bytes 12582920 | tf_op jit(solution)/shard_map/ppermute | solution.py:380
  43.0 13.1 %collective-permute-start.8 = (bf16[128,1024]{1,0:T(8,128)(2,1)S(1)}, bf16[128,1024]{1,0:T(8,128)(2,1)S(1)}, u32[]{:S(2)}, u32[]{:S(2)}) collective-permute-start(bf16[128,1024]{1,0:T(8,128)(2,1)S(1)} %multiply_convert_fusion.2), channel_id=1, source_target_pairs={{0,2},{1,3},{2,0},{3,1},{4,6},{5,7},{6,4},{7,5},{8,10},{9,11},{10,... | collective-permute-start | bytes 786440 | tf_op jit(solution)/shard_map/ppermute | solution.py:23
  56.3 24.4 %collective-permute-start.11 = (bf16[512,1024]{1,0:T(8,128)(2,1)S(1)}, bf16[512,1024]{1,0:T(8,128)(2,1)S(1)}, u32[]{:S(2)}, u32[]{:S(2)}) collective-permute-start(bf16[512,1024]{1,0:T(8,128)(2,1)S(1)} %pad_maximum_fusion.refs_1_), channel_id=1, source_target_pairs={{28,0},{0,4},{4,8},{8,12},{12,16},{16,20},{20,24},{24,28},{29,1},{... | collective-permute-start | bytes 3145736 | tf_op jit(solution)/shard_map/ppermute | solution.py:380
  58.5 14.4 %collective-permute-start.1 = (bf16[128,1024]{1,0:T(8,128)(2,1)S(1)}, bf16[128,1024]{1,0:T(8,128)(2,1)S(1)}, u32[]{:S(2)}, u32[]{:S(2)}) collective-permute-start(bf16[128,1024]{1,0:T(8,128)(2,1)S(1)} %get-tuple-element.105.refs_0_.refs_4_), channel_id=1, source_target_pairs={{0,1},{1,0},{2,3},{3,2},{4,5},{5,4},{6,7},{7,6},{8,9},{9,8},{10,11... | collective-permute-start | bytes 786440 | tf_op jit(solution)/shard_map/ppermute | solution.py:23
  59.9 14.7 %collective-permute-start.2 = (bf16[128,1024]{1,0:T(8,128)(2,1)S(1)}, bf16[128,1024]{1,0:T(8,128)(2,1)S(1)}, u32[]{:S(2)}, u32[]{:S(2)}) collective-permute-start(bf16[128,1024]{1,0:T(8,128)(2,1)S(1)} %get-tuple-element.105.refs_0_.refs_4_), channel_id=1, source_target_pairs={{0,2},{1,3},{2,0},{3,1},{4,6},{5,7},{6,4},{7,5},{8,10},{9,11},{10,... | collective-permute-start | bytes 786440 | tf_op jit(solution)/shard_map/ppermute | solution.py:23
  60.5 14.1 %collective-permute-start.3 = (bf16[128,1024]{1,0:T(8,128)(2,1)S(1)}, bf16[128,1024]{1,0:T(8,128)(2,1)S(1)}, u32[]{:S(2)}, u32[]{:S(2)}) collective-permute-start(bf16[128,1024]{1,0:T(8,128)(2,1)S(1)} %get-tuple-element.105.refs_0_.refs_4_), channel_id=1, source_target_pairs={{0,3},{1,2},{2,1},{3,0},{4,7},{5,6},{6,5},{7,4},{8,11},{9,10},{10,... | collective-permute-start | bytes 786440 | tf_op jit(solution)/shard_map/ppermute | solution.py:23
  81.7 58.3 %collective-permute-start.18 = (bf16[2,1024,1024]{2,1,0:T(8,128)(2,1)}, bf16[2,1024,1024]{2,1,0:T(8,128)(2,1)}, u32[]{:S(2)}, u32[]{:S(2)}) collective-permute-start(bf16[2,1024,1024]{2,1,0:T(8,128)(2,1)} %shard_map.91), channel_id=1, source_target_pairs={{24,0},{0,8},{8,16},{16,24},{25,1},{1,9},{9,17},{17,25},{26,2},{2,... | collective-permute-start | bytes 12582920 | tf_op jit(solution)/shard_map/ppermute | solution.py:380
  110.2 13.0 %collective-permute-start.13 = (bf16[128,1024]{1,0:T(8,128)(2,1)}, bf16[128,1024]{1,0:T(8,128)(2,1)S(1)}, u32[]{:S(2)}, u32[]{:S(2)}) collective-permute-start(bf16[128,1024]{1,0:T(8,128)(2,1)} %get-tuple-element.64), channel_id=1, source_target_pairs={{0,2},{1,3},{2,0},{3,1},{4,6},{5,7},{6,4},{7,5},{8,10},{9,11},{10,... | collective-permute-start | bytes 786440 | tf_op jit(solution)/shard_map/ppermute | solution.py:23
  125.9 13.4 %collective-permute-start.16 = (bf16[128,1024]{1,0:T(8,128)(2,1)S(1)}, bf16[128,1024]{1,0:T(8,128)(2,1)S(1)}, u32[]{:S(2)}, u32[]{:S(2)}) collective-permute-start(bf16[128,1024]{1,0:T(8,128)(2,1)S(1)} %multiply_convert_fusion.1), channel_id=1, source_target_pairs={{0,2},{1,3},{2,0},{3,1},{4,6},{5,7},{6,4},{7,5},{8,10},{9,11},{10,... | collective-permute-start | bytes 786440 | tf_op jit(solution)/shard_map/ppermute | solution.py:23
  139.3 15.3 %collective-permute-start.19 = (bf16[512,1024]{1,0:T(8,128)(2,1)S(1)}, bf16[512,1024]{1,0:T(8,128)(2,1)S(1)}, u32[]{:S(2)}, u32[]{:S(2)}) collective-permute-start(bf16[512,1024]{1,0:T(8,128)(2,1)S(1)} %pad_maximum_fusion.1.refs_2_), channel_id=1, source_target_pairs={{28,4},{4,12},{12,20},{20,28},{29,5},{5,13},{13,21},{21,29},{30,6}... | collective-permute-start | bytes 3145736 | tf_op jit(solution)/shard_map/ppermute | solution.py:380
  155.7 52.5 %collective-permute-start.28 = (bf16[2,1024,1024]{2,1,0:T(8,128)(2,1)}, bf16[2,1024,1024]{2,1,0:T(8,128)(2,1)}, u32[]{:S(2)}, u32[]{:S(2)}) collective-permute-start(bf16[2,1024,1024]{2,1,0:T(8,128)(2,1)} %shard_map.93.refs_1_.refs_2_), channel_id=1, source_target_pairs={{24,0},{0,8},{8,16},{16,24},{25,1},{1,9},{9,17},{17,25},{26,2},{2,... | collective-permute-start | bytes 12582920 | tf_op jit(solution)/shard_map/ppermute | solution.py:380
  164.5 13.9 %collective-permute-start.22 = (bf16[128,1024]{1,0:T(8,128)(2,1)S(1)}, bf16[128,1024]{1,0:T(8,128)(2,1)S(1)}, u32[]{:S(2)}, u32[]{:S(2)}) collective-permute-start(bf16[128,1024]{1,0:T(8,128)(2,1)S(1)} %collective-permute-done.20.refs_0_.refs_4_), channel_id=1, source_target_pairs={{0,2},{1,3},{2,0},{3,1},{4,6},{5,7},{6,4},{7,5},{8,10},{9,11},{10,... | collective-permute-start | bytes 786440 | tf_op jit(solution)/shard_map/ppermute | solution.py:23
  166.0 15.1 %collective-permute-start.23 = (bf16[128,1024]{1,0:T(8,128)(2,1)S(1)}, bf16[128,1024]{1,0:T(8,128)(2,1)S(1)}, u32[]{:S(2)}, u32[]{:S(2)}) collective-permute-start(bf16[128,1024]{1,0:T(8,128)(2,1)S(1)} %collective-permute-done.20.refs_0_.refs_4_), channel_id=1, source_target_pairs={{0,3},{1,2},{2,1},{3,0},{4,7},{5,6},{6,5},{7,4},{8,11},{9,10},{10,... | collective-permute-start | bytes 786440 | tf_op jit(solution)/shard_map/ppermute | solution.py:23
  171.9 14.8 %collective-permute-start.24 = (bf16[1024,1024]{1,0:T(8,128)(2,1)}, bf16[1024,1024]{1,0:T(8,128)(2,1)}, u32[]{:S(2)}, u32[]{:S(2)}) collective-permute-start(bf16[1024,1024]{1,0:T(8,128)(2,1)} %shard_map.95), channel_id=1, source_target_pairs={{0,4},{8,12},{16,20},{24,28},{1,5},{9,13},{17,21},{25,29},{2,6},{1... | collective-permute-start | bytes 6291464 | tf_op jit(solution)/shard_map/ppermute | solution.py:380
  235.8 13.6 %collective-permute-start.33 = (bf16[128,1024]{1,0:T(8,128)(2,1)S(1)}, bf16[128,1024]{1,0:T(8,128)(2,1)S(1)}, u32[]{:S(2)}, u32[]{:S(2)}) collective-permute-start(bf16[128,1024]{1,0:T(8,128)(2,1)S(1)} %multiply_convert_fusion.refs_2_), channel_id=1, source_target_pairs={{0,2},{1,3},{2,0},{3,1},{4,6},{5,7},{6,4},{7,5},{8,10},{9,11},{10,... | collective-permute-start | bytes 786440 | tf_op jit(solution)/shard_map/ppermute | solution.py:23
  236.5 12.9 %collective-permute-start.34 = (bf16[128,1024]{1,0:T(8,128)(2,1)S(1)}, bf16[128,1024]{1,0:T(8,128)(2,1)S(1)}, u32[]{:S(2)}, u32[]{:S(2)}) collective-permute-start(bf16[128,1024]{1,0:T(8,128)(2,1)S(1)} %multiply_convert_fusion.refs_2_), channel_id=1, source_target_pairs={{0,3},{1,2},{2,1},{3,0},{4,7},{5,6},{6,5},{7,4},{8,11},{9,10},{10,... | collective-permute-start | bytes 786440 | tf_op jit(solution)/shard_map/ppermute | solution.py:23
  270.6 15.7 %collective-permute-start.40 = (bf16[256,1024]{1,0:T(8,128)(2,1)S(1)}, bf16[256,1024]{1,0:T(8,128)(2,1)S(1)}, u32[]{:S(2)}, u32[]{:S(2)}) collective-permute-start(bf16[256,1024]{1,0:T(8,128)(2,1)S(1)} %get-tuple-element.99), channel_id=1, source_target_pairs={{0,8},{4,12},{24,16},{28,20},{1,9},{5,13},{25,17},{29,21},{2,10},{... | collective-permute-start | bytes 1572872 | tf_op jit(solution)/shard_map/ppermute | solution.py:316
  274.1 23.4 %collective-permute-start.39 = (bf16[256,1024]{1,0:T(8,128)(2,1)S(1)}, bf16[256,1024]{1,0:T(8,128)(2,1)S(1)}, u32[]{:S(2)}, u32[]{:S(2)}) collective-permute-start(bf16[256,1024]{1,0:T(8,128)(2,1)S(1)} %get-tuple-element.100), channel_id=1, source_target_pairs={{0,8},{4,12},{24,16},{28,20},{1,9},{5,13},{25,17},{29,21},{2,10},{... | collective-permute-start | bytes 1572872 | tf_op jit(solution)/shard_map/ppermute | solution.py:316
  287.3 22.6 %collective-permute-start.37 = (bf16[256,1024]{1,0:T(8,128)(2,1)S(1)}, bf16[256,1024]{1,0:T(8,128)(2,1)S(1)}, u32[]{:S(2)}, u32[]{:S(2)}) collective-permute-start(bf16[256,1024]{1,0:T(8,128)(2,1)S(1)} %get-tuple-element.104), channel_id=1, source_target_pairs={{0,8},{4,12},{24,16},{28,20},{1,9},{5,13},{25,17},{29,21},{2,10},{... | collective-permute-start | bytes 1572872 | tf_op jit(solution)/shard_map/ppermute | solution.py:316
  300.4 24.7 %collective-permute-start.36 = (bf16[256,1024]{1,0:T(8,128)(2,1)S(1)}, bf16[256,1024]{1,0:T(8,128)(2,1)S(1)}, u32[]{:S(2)}, u32[]{:S(2)}) collective-permute-start(bf16[256,1024]{1,0:T(8,128)(2,1)S(1)} %get-tuple-element.103), channel_id=1, source_target_pairs={{0,8},{4,12},{24,16},{28,20},{1,9},{5,13},{25,17},{29,21},{2,10},{... | collective-permute-start | bytes 1572872 | tf_op jit(solution)/shard_map/ppermute | solution.py:316
  308.5 15.4 %collective-permute-start.48 = (bf16[256,1024]{1,0:T(8,128)(2,1)}, bf16[256,1024]{1,0:T(8,128)(2,1)}, u32[]{:S(2)}, u32[]{:S(2)}) collective-permute-start(bf16[256,1024]{1,0:T(8,128)(2,1)} %fusion.4.refs_1_), channel_id=1, source_target_pairs={{8,0},{12,4},{16,24},{20,28},{9,1},{13,5},{17,25},{21,29},{10,2},{... | collective-permute-start | bytes 1572872 | tf_op jit(solution)/shard_map/ppermute | solution.py:316
  313.1 21.0 %collective-permute-start.47 = (bf16[256,1024]{1,0:T(8,128)(2,1)}, bf16[256,1024]{1,0:T(8,128)(2,1)S(1)}, u32[]{:S(2)}, u32[]{:S(2)}) collective-permute-start(bf16[256,1024]{1,0:T(8,128)(2,1)} %fusion.5.refs_1_), channel_id=1, source_target_pairs={{8,0},{12,4},{16,24},{20,28},{9,1},{13,5},{17,25},{21,29},{10,2},{... | collective-permute-start | bytes 1572872 | tf_op jit(solution)/shard_map/ppermute | solution.py:316
  335.5 24.1 %collective-permute-start.46 = (bf16[256,1024]{1,0:T(8,128)(2,1)S(1)}, bf16[256,1024]{1,0:T(8,128)(2,1)S(1)}, u32[]{:S(2)}, u32[]{:S(2)}) collective-permute-start(bf16[256,1024]{1,0:T(8,128)(2,1)S(1)} %copy-done.3), channel_id=1, source_target_pairs={{8,0},{12,4},{16,24},{20,28},{9,1},{13,5},{17,25},{21,29},{10,2},{... | collective-permute-start | bytes 1572872 | tf_op jit(solution)/shard_map/ppermute | solution.py:316
  337.0 33.6 %collective-permute-start.45 = (bf16[256,1024]{1,0:T(8,128)(2,1)S(1)}, bf16[256,1024]{1,0:T(8,128)(2,1)S(1)}, u32[]{:S(2)}, u32[]{:S(2)}) collective-permute-start(bf16[256,1024]{1,0:T(8,128)(2,1)S(1)} %fusion.7), channel_id=1, source_target_pairs={{8,0},{12,4},{16,24},{20,28},{9,1},{13,5},{17,25},{21,29},{10,2},{... | collective-permute-start | bytes 1572872 | tf_op jit(solution)/shard_map/ppermute | solution.py:316
  (57 other events, 420.8 us)

commit v2 on v1

--- a/solution.py
+++ b/solution.py
@@ -329,7 +329,8 @@
     for c in range(chunks):
         p, start = divmod(c * size, pair_rows)
         blocks.append(added(mine[c * size : (c + 1) * size], pairs[p][start : start + size]))
-    arrived, results, tokens = {}, [], []
+    arrived, made, results, tokens = {}, {}, [], []
+    final = len(stages) - 1
     for tick in range(chunks + len(stages)):
         for s in reversed(range(len(stages) + 1)):
             c = tick - s
@@ -340,11 +341,11 @@
                 adds, hops = stages[s - 1]
                 fresh = added(block, arrived[s - 1, c]) if adds else arrived[s - 1, c]
                 block = jnp.where(at([b for _, b in hops]), fresh, block)
-                if s == len(stages) and c:
+                if s > final and c:
                     block = tied([tokens[c - 1]], block)
-                if s == 1 and c:
-                    block = tied([blocks[c - 1]], block)
-            blocks[c] = block
+            if s == 0 and c >= 3 and (2, c - 3) in made:
+                block = tied([made[2, c - 3]], block)
+            blocks[c] = made[s, c] = block
             if s < len(stages):
                 arrived[s, c] = moved(block, stages[s][1])
             else:
@@ -382,16 +383,15 @@
     def picked(step, count):
         return tokens.at[picks_all[step, :count]].get(mode="promise_in_bounds")
 
-    shares = jnp.concatenate([picks_all[step, :share_rows] for step in range(2)])
-    shares = sent(tokens.at[shares].get(mode="promise_in_bounds"), 1)
-    near_share, far_share = shares[:share_rows], shares[share_rows:]
-    narrow = tied([shares], momentum[0].astype(bf16))
+    near_share = sent(picked(0, share_rows), 1)
+    narrow = tied([near_share], momentum[0].astype(bf16))
     moment_near = sent(narrow, 1)
 
     inputs = [picked(0, row_count)]
     hidden, slope, *partials = forward(flag, inputs, [anchor], only, tensors, emits=False, waits=[narrow])
     error = jnp.concatenate(gathered(error_share(partials, 0)))
     error_near = sent(error, 1)
+    inputs_next = picked(1, row_count)
     moment, moment_bf = backward(
         flag,
         [error],
@@ -402,6 +402,7 @@
         [momentum[0]],
         first_update,
         [f32, bf16],
+        waits=[inputs_next],
     )
     inputs_near = gathered(near_share)
     hidden_near, slope_near = forward(flag, inputs_near, [anchor], only, 0, emits=False, waits=[moment])
@@ -418,7 +419,8 @@
         [(bf16, 2), bf16],
     )
 
-    inputs = [picked(1, row_count)]
+    inputs = [tied([moment_near[0]], inputs_next)]
+    inputs_far = sent(inputs[0], 2, (1,))
     hidden, slope, *partials = forward(flag, inputs, [weights], only, tensors, emits=False)
     error = jnp.concatenate(gathered(error_share(partials, 1)))
     error_far = sent(error, 2, (1,))
@@ -434,14 +436,13 @@
         [f32, bf16, bf16],
         waits=[moment_far],
     )
-    weights = tied([error_far], weights)
+    weights = tied([error_far[:16], inputs_far[:16]], weights)
     weights_sent = sent(weights, 2, (0,))
-    inputs_far = gathered(sent(tied([weights], far_share), 1, (1,)))
     moment_two = tuple(sent(tied([weights], part), 1, (1,)) for part in moment_near)
     moment_three = tuple(sent(tied([weights], moment_far[k]), 1, (1,)) for k in range(2))
-    hidden, slope, weights_far = forward(flag, inputs_far, [anchor, moment_two, moment_three], pushed, 0)
+    hidden, slope, weights_far = forward(flag, [inputs_far], [anchor, moment_two, moment_three], pushed, 0)
     (weights_found,) = backward(
-        flag, [error_far], weights_far, slope, hidden, inputs_far, [moment_two, weights_far], second_beside, [bf16]
+        flag, [error_far], weights_far, slope, hidden, [inputs_far], [moment_two, weights_far], second_beside, [bf16]
     )
 
     inputs = [picked(2, row_count)]

time: 391 us -> 382 us (0.977)
  waiting for transfers between devices: 129 us -> 119 us
    ppermute x11, starting transfers between devices: 23.2 us -> 29.4 us  [sent(): return lax.ppermute(block, 'replica', route)]
    ppermute x12, waiting for transfers between devices: 50.7 us -> 46.3 us  [moved(): lax.ppermute(part, axis, [(cores * a + c, cores * b + c) for a, b in hops...]
    select_n x12, other arithmetic: 12.6 us -> 8.36 us  [slow_step(): block = jnp.where(at([b for _, b in hops]), fresh, block)]
    ppermute x30 -> x27, starting transfers between devices: 29.4 us -> 25.5 us  [swapped(): lax.ppermute(block, axis, [(i, i ^ mask) for i in range(lax.axis_size(axi...]
    ppermute x30 -> x27, waiting for transfers between devices: 73.4 us -> 70.3 us  [swapped(): lax.ppermute(block, axis, [(i, i ^ mask) for i in range(lax.axis_size(axi...]
    gather x3 -> x4, local copies, waits for them, and re-layouts: 8.38 us -> 9.26 us  [picked(): return tokens.at[picks_all[step, :count]].get(mode='promise_in_bounds')]
    unnamed x56 -> x42, local copies, waits for them, and re-layouts: 7.94 us -> 8.43 us
  transfers between devices with their start and end apart: 53 -> 50, of which waited for: 27 -> 27; matrix products, arithmetic and copies ran while one was open for 10% -> 9% of each run, Pallas kernels for 23% -> 24%
where the time goes in v2:
time: 382 us; the launch traced here: 375 us
  Pallas kernels  123 us (32%)
  waiting for transfers between devices  119 us (31%)
  starting transfers between devices  81.3 us (21%)
  local copies, waits for them, and re-layouts  27.5 us (7%)
  other arithmetic  22.8 us (6%)
    ppermute x27, waiting for transfers between devices, swapped(): lax.ppermute(block, axis, [(i, i ^ mask) for i in range(lax.axis_size(axi...  70.3 us
    pallas_call x5, Pallas kernels, backward(): pl.pallas_call(functools.partial(backward_kernel, update, counts, (len(er...  62.6 us
    ppermute x12, waiting for transfers between devices, moved(): lax.ppermute(part, axis, [(cores * a + c, cores * b + c) for a, b in hops...  46.3 us
    pallas_call x5, Pallas kernels, forward(): pl.pallas_call(functools.partial(forward_kernel, mix, counts, len(inputs)...  43.5 us
    ppermute x11, starting transfers between devices, sent(): return lax.ppermute(block, 'replica', route)  29.4 us
    ppermute x12, starting transfers between devices, moved(): lax.ppermute(part, axis, [(cores * a + c, cores * b + c) for a, b in hops...  26.4 us
    ppermute x27, starting transfers between devices, swapped(): lax.ppermute(block, axis, [(i, i ^ mask) for i in range(lax.axis_size(axi...  25.5 us
    pallas_call x4, Pallas kernels, finish(): pl.pallas_call(functools.partial(finish_kernel, replicas), grid=(steps,),...  16.5 us
  transfers between devices with their start and end apart: 50, of which 27 were waited for; matrix products, arithmetic and copies ran while one was open for 9% of the time, Pallas kernels for 24%

profile of v2, /device:TPU:0, one launch (start us, length us, event | category | flops | bytes accessed | tf_op | source)
XLA Modules:
  0.0 374.8 jit_solution(8953201614463162600)
XLA Ops:
  3.4 6.1 %bitcast_convert_fusion.refs_0_ = bf16[2,1024,1024]{2,1,0:T(8,128)(2,1)} fusion(f32[1,2,1024,1024]{3,2,1,0:T(8,128)} %param.10), kind=kLoop, calls=%fused_computation.63 | loop fusion | flops 2097152 | bytes 12582912 | tf_op jit(solution)/shard_map/convert_element_type | solution.py:387
  15.7 9.0 %shard_map.86 = (bf16[512,1024]{1,0:T(8,128)(2,1)}, bf16[512,1024]{1,0:T(8,128)(2,1)}, bf16[128,1024]{1,0:T(8,128)(2,1)}, bf16[128,1024]{1,0:T(8,128)(2,1)}, bf1...) custom-call(s32[1]{0:T(128)} %bitcast.flag, bf16[512,1024]{1,0:T(8,128)(2,1)} %gather_fusion.4, ...), custom_call_target="tpu_custom_call" | custom-call | flops 1 | bytes 1 | tf_op jit(solution)/shard_map/pallas_call | solution.py:124
  29.1 6.0 %collective-permute-done.6 = bf16[128,1024]{1,0:T(8,128)(2,1)S(1)} collective-permute-done((bf16[128,1024]{1,0:T(8,128)(2,1)}, bf16[128,1024]{1,0:T(8,128)(2,1)S(1)}, u32[]{:S(2)}, u32[]{:S(2)}) %collective-permute-start.6) | collective-permute-done | bytes 262176 | tf_op jit(solution)/shard_map/ppermute | solution.py:23
  45.3 6.6 %collective-permute-done.9 = bf16[128,1024]{1,0:T(8,128)(2,1)S(1)} collective-permute-done((bf16[128,1024]{1,0:T(8,128)(2,1)S(1)}, bf16[128,1024]{1,0:T(8,128)(2,1)S(1)}, u32[]{:S(2)}, u32[]{:S(2)}) %collective-permute-start.9) | collective-permute-done | bytes 262176 | tf_op jit(solution)/shard_map/ppermute | solution.py:23
  64.1 10.9 %shard_map.87 = (f32[2,1024,1024]{2,1,0:T(8,128)}, bf16[2,1024,1024]{2,1,0:T(8,128)(2,1)}) custom-call(s32[1]{0:T(128)} %bitcast.flag, f32[2,1024,1024]{2,1,0:T(8,128)} %anchor.7, bf16[512,1024]{1,0:T(8,128)(2,1)} %get-tuple-element.50.slope, bf16[512,1024]{1,0:T(8,128)(2,1)} %get-tuple-element.51.hidden, f32[2,1024,1024]{2,1,0:T(8,128)} %bitcast.47, ...), custom_call_target="tpu_custom_call" | custom-call | flops 1 | bytes 1 | tf_op jit(solution)/shard_map/pallas_call | solution.py:208
  85.1 13.5 %shard_map.89 = (bf16[1024,1024]{1,0:T(8,128)(2,1)}, bf16[1024,1024]{1,0:T(8,128)(2,1)}, bf16[2,1024,1024]{2,1,0:T(8,128)(2,1)}) custom-call(s32[1]{0:T(128)} %bitcast.flag, f32[2,1024,1024]{2,1,0:T(8,128)} %anchor.7, bf16[512,1024]{1,0:T(8,128)(2,1)} %get-tuple-element.57.slope, bf16[512,1024]{1,0:T(8,128)(2,1)} %get-tuple-element.58.hidden.refs_2_, ...), custom_call_target="tpu_custom_call" | custom-call | flops 1 | bytes 1 | tf_op jit(solution)/shard_map/pallas_call | solution.py:208
  98.6 7.1 %shard_map.91 = (bf16[512,1024]{1,0:T(8,128)(2,1)}, bf16[512,1024]{1,0:T(8,128)(2,1)}, bf16[128,1024]{1,0:T(8,128)(2,1)}, bf16[128,1024]{1,0:T(8,128)(2,1)}, bf1...) custom-call(s32[1]{0:T(128)} %bitcast.flag, bf16[512,1024]{1,0:T(8,128)(2,1)} %shard_map.90.refs_0_.refs_3_, ...), custom_call_target="tpu_custom_call" | custom-call | flops 1 | bytes 1 | tf_op jit(solution)/shard_map/pallas_call | solution.py:124
  110.1 6.1 %collective-permute-done.15 = bf16[128,1024]{1,0:T(8,128)(2,1)} collective-permute-done((bf16[128,1024]{1,0:T(8,128)(2,1)}, bf16[128,1024]{1,0:T(8,128)(2,1)}, u32[]{:S(2)}, u32[]{:S(2)}) %collective-permute-start.15) | collective-permute-done | bytes 262176 | tf_op jit(solution)/shard_map/ppermute | solution.py:23
  126.5 5.9 %collective-permute-done.18 = bf16[128,1024]{1,0:T(8,128)(2,1)S(1)} collective-permute-done((bf16[128,1024]{1,0:T(8,128)(2,1)S(1)}, bf16[128,1024]{1,0:T(8,128)(2,1)S(1)}, u32[]{:S(2)}, u32[]{:S(2)}) %collective-permute-start.18) | collective-permute-done | bytes 262176 | tf_op jit(solution)/shard_map/ppermute | solution.py:23
  139.6 14.4 %shard_map.93 = (f32[2,1024,1024]{2,1,0:T(8,128)}, bf16[2,1024,1024]{2,1,0:T(8,128)(2,1)}, bf16[2,1024,1024]{2,1,0:T(8,128)(2,1)}) custom-call(s32[1]{0:T(128)} %bitcast.flag, bf16[2,1024,1024]{2,1,0:T(8,128)(2,1)} %get-tuple-element.60.refs_1_.weights, bf16[512,1024]{1,0:T(8,128)(2,1)} %get-tuple-element.61.slope, ...), custom_call_target="tpu_custom_call" | custom-call | flops 1 | bytes 1 | tf_op jit(solution)/shard_map/pallas_call | solution.py:208
  163.7 9.4 %collective-permute-start.21 = (bf16[1024,1024]{1,0:T(8,128)(2,1)}, bf16[1024,1024]{1,0:T(8,128)(2,1)}, u32[]{:S(2)}, u32[]{:S(2)}) collective-permute-start(bf16[1024,1024]{1,0:T(8,128)(2,1)} %shard_map.95), channel_id=1, source_target_pairs={{0,4},{8,12},{16,20},{24,28},{1,5},{9,13},{17,21},{25,29},{2,6},{1... | collective-permute-start | bytes 6291464 | tf_op jit(solution)/shard_map/ppermute | solution.py:381
  184.9 11.2 %shard_map.99 = (bf16[512,1024]{1,0:T(8,128)(2,1)}, bf16[512,1024]{1,0:T(8,128)(2,1)}, bf16[2,1024,1024]{2,1,0:T(8,128)(2,1)}) custom-call(s32[1]{0:T(128)} %bitcast.flag, bf16[512,1024]{1,0:T(8,128)(2,1)} %copy-done.5, f32[2,1024,1024]{2,1,0:T(8,128)} %anchor.7, bf16[1024,1024]{1,0:T(8,128)(2,1)} %collective-permute-done.21.refs_2_.refs_0_, ...), custom_call_target="tpu_custom_call" | custom-call | flops 1 | bytes 1 | tf_op jit(solution)/shard_map/pallas_call | solution.py:124
  196.2 10.3 %shard_map.100.refs_1_ = bf16[2,1024,1024]{2,1,0:T(8,128)(2,1)} custom-call(s32[1]{0:T(128)} %bitcast.flag, bf16[2,1024,1024]{2,1,0:T(8,128)(2,1)} %get-tuple-element.70.weights.refs_2_, bf16[512,1024]{1,0:T(8,128)(2,1)} %get-tuple-element.71.slope, bf16[512,1024]{1,0:T(8,128)(2,1)} %get-tuple-element.72.hidden, ...), custom_call_target="tpu_custom_call" | custom-call | flops 1 | bytes 1 | tf_op jit(solution)/shard_map/pallas_call | solution.py:208
  208.0 10.8 %shard_map.101 = (bf16[512,1024]{1,0:T(8,128)(2,1)}, bf16[512,1024]{1,0:T(8,128)(2,1)}, bf16[128,1024]{1,0:T(8,128)(2,1)}, bf16[128,1024]{1,0:T(8,128)(2,1)}, bf...) custom-call(s32[1]{0:T(128)} %bitcast.flag, bf16[512,1024]{1,0:T(8,128)(2,1)} %gather_fusion.1, ...), custom_call_target="tpu_custom_call" | custom-call | flops 1 | bytes 1 | tf_op jit(solution)/shard_map/pallas_call | solution.py:124
  223.2 6.0 %collective-permute-done.28 = bf16[128,1024]{1,0:T(8,128)(2,1)S(1)} collective-permute-done((bf16[128,1024]{1,0:T(8,128)(2,1)}, bf16[128,1024]{1,0:T(8,128)(2,1)S(1)}, u32[]{:S(2)}, u32[]{:S(2)}) %collective-permute-start.28) | collective-permute-done | bytes 262176 | tf_op jit(solution)/shard_map/ppermute | solution.py:23
  243.2 5.8 %collective-permute-done.30.refs_4_ = bf16[128,1024]{1,0:T(8,128)(2,1)S(1)} collective-permute-done((bf16[128,1024]{1,0:T(8,128)(2,1)S(1)}, bf16[128,1024]{1,0:T(8,128)(2,1)S(1)}, u32[]{:S(2)}, u32[]{:S(2)}) %collective-permute-start.30) | collective-permute-done | bytes 262176 | tf_op jit(solution)/shard_map/ppermute | solution.py:23
  249.8 13.6 %shard_map.102 = (f32[2,1024,1024]{2,1,0:T(8,128)}, bf16[1024,1024]{1,0:T(8,128)(2,1)}, bf16[512,1024]{1,0:T(8,128)(2,1)}, bf16[512,1024]{1,0:T(8,128)(2,1)}) custom-call(s32[1]{0:T(128)} %bitcast.flag, bf16[2,1024,1024]{2,1,0:T(8,128)(2,1)} %get-tuple-element.73.weights, bf16[512,1024]{1,0:T(8,128)(2,1)} %get-tuple-element.74.slope, ...), custom_call_target="tpu_custom_call" | custom-call | flops 1 | bytes 1 | tf_op jit(solution)/shard_map/pallas_call | solution.py:208
  274.9 10.1 %collective-permute-done.34 = bf16[256,1024]{1,0:T(8,128)(2,1)S(1)} collective-permute-done((bf16[256,1024]{1,0:T(8,128)(2,1)S(1)}, bf16[256,1024]{1,0:T(8,128)(2,1)S(1)}, u32[]{:S(2)}, u32[]{:S(2)}) %collective-permute-start.34) | collective-permute-done | bytes 524320 | tf_op jit(solution)/shard_map/ppermute | solution.py:316
  286.7 6.4 %collective-permute-start.39 = (bf16[256,1024]{1,0:T(8,128)(2,1)S(1)}, bf16[256,1024]{1,0:T(8,128)(2,1)S(1)}, u32[]{:S(2)}, u32[]{:S(2)}) collective-permute-start(bf16[256,1024]{1,0:T(8,128)(2,1)S(1)} %get-tuple-element.104), channel_id=1, source_target_pairs={{0,8},{4,12},{24,16},{28,20},{1,9},{5,13},{25,17},{29,21},{2,10},{... | collective-permute-start | bytes 1572872 | tf_op jit(solution)/shard_map/ppermute | solution.py:316
  300.2 7.4 %collective-permute-start.36 = (bf16[256,1024]{1,0:T(8,128)(2,1)}, bf16[256,1024]{1,0:T(8,128)(2,1)S(1)}, u32[]{:S(2)}, u32[]{:S(2)}) collective-permute-start(bf16[256,1024]{1,0:T(8,128)(2,1)} %shard_map.103), channel_id=1, source_target_pairs={{0,8},{4,12},{24,16},{28,20},{1,9},{5,13},{25,17},{29,21},{2,10},{... | collective-permute-start | bytes 1572872 | tf_op jit(solution)/shard_map/ppermute | solution.py:316
  311.4 6.6 %collective-permute-done.36 = bf16[256,1024]{1,0:T(8,128)(2,1)S(1)} collective-permute-done((bf16[256,1024]{1,0:T(8,128)(2,1)}, bf16[256,1024]{1,0:T(8,128)(2,1)S(1)}, u32[]{:S(2)}, u32[]{:S(2)}) %collective-permute-start.36) | collective-permute-done | bytes 524320 | tf_op jit(solution)/shard_map/ppermute | solution.py:316
  320.2 7.8 %collective-permute-done.45 = bf16[256,1024]{1,0:T(8,128)(2,1)S(1)} collective-permute-done((bf16[256,1024]{1,0:T(8,128)(2,1)}, bf16[256,1024]{1,0:T(8,128)(2,1)S(1)}, u32[]{:S(2)}, u32[]{:S(2)}) %collective-permute-start.45) | collective-permute-done | bytes 524320 | tf_op jit(solution)/shard_map/ppermute | solution.py:316
  329.6 9.6 %collective-permute-done.44 = bf16[256,1024]{1,0:T(8,128)(2,1)S(1)} collective-permute-done((bf16[256,1024]{1,0:T(8,128)(2,1)S(1)}, bf16[256,1024]{1,0:T(8,128)(2,1)S(1)}, u32[]{:S(2)}, u32[]{:S(2)}) %collective-permute-start.44) | collective-permute-done | bytes 524320 | tf_op jit(solution)/shard_map/ppermute | solution.py:316
  353.7 7.7 %collective-permute-done.38 = bf16[256,1024]{1,0:T(8,128)(2,1)S(1)} collective-permute-done((bf16[256,1024]{1,0:T(8,128)(2,1)S(1)}, bf16[256,1024]{1,0:T(8,128)(2,1)S(1)}, u32[]{:S(2)}, u32[]{:S(2)}) %collective-permute-start.38) | collective-permute-done | bytes 524320 | tf_op jit(solution)/shard_map/ppermute | solution.py:316
  (185 shorter events, 165.0 us)
Async XLA Ops:
  13.0 72.0 %collective-permute-start.10 = (bf16[2,1024,1024]{2,1,0:T(8,128)(2,1)}, bf16[2,1024,1024]{2,1,0:T(8,128)(2,1)}, u32[]{:S(2)}, u32[]{:S(2)}) collective-permute-start(bf16[2,1024,1024]{2,1,0:T(8,128)(2,1)} %shard_map.85.refs_2_), channel_id=1, source_target_pairs={{28,0},{0,4},{4,8},{8,12},{12,16},{16,20},{20,24},{24,28},{29,1},{... | collective-permute-start | bytes 12582920 | tf_op jit(solution)/shard_map/ppermute | solution.py:381
  43.5 13.1 %collective-permute-start.8 = (bf16[128,1024]{1,0:T(8,128)(2,1)S(1)}, bf16[128,1024]{1,0:T(8,128)(2,1)S(1)}, u32[]{:S(2)}, u32[]{:S(2)}) collective-permute-start(bf16[128,1024]{1,0:T(8,128)(2,1)S(1)} %multiply_convert_fusion.2), channel_id=1, source_target_pairs={{0,2},{1,3},{2,0},{3,1},{4,6},{5,7},{6,4},{7,5},{8,10},{9,11},{10,... | collective-permute-start | bytes 786440 | tf_op jit(solution)/shard_map/ppermute | solution.py:23
  57.8 22.6 %collective-permute-start.11 = (bf16[512,1024]{1,0:T(8,128)(2,1)}, bf16[512,1024]{1,0:T(8,128)(2,1)S(1)}, u32[]{:S(2)}, u32[]{:S(2)}) collective-permute-start(bf16[512,1024]{1,0:T(8,128)(2,1)} %pad_maximum_fusion.refs_1_), channel_id=1, source_target_pairs={{28,0},{0,4},{4,8},{8,12},{12,16},{16,20},{20,24},{24,28},{29,1},{... | collective-permute-start | bytes 3145736 | tf_op jit(solution)/shard_map/ppermute | solution.py:381
  57.8 17.2 %collective-permute-start.1 = (bf16[128,1024]{1,0:T(8,128)(2,1)S(1)}, bf16[128,1024]{1,0:T(8,128)(2,1)}, u32[]{:S(2)}, u32[]{:S(2)}) collective-permute-start(bf16[128,1024]{1,0:T(8,128)(2,1)S(1)} %copy-done.9), channel_id=1, source_target_pairs={{0,1},{1,0},{2,3},{3,2},{4,5},{5,4},{6,7},{7,6},{8,9},{9,8},{10,11... | collective-permute-start | bytes 786440 | tf_op jit(solution)/shard_map/ppermute | solution.py:23
  59.3 15.7 %collective-permute-start.2 = (bf16[128,1024]{1,0:T(8,128)(2,1)S(1)}, bf16[128,1024]{1,0:T(8,128)(2,1)}, u32[]{:S(2)}, u32[]{:S(2)}) collective-permute-start(bf16[128,1024]{1,0:T(8,128)(2,1)S(1)} %copy-done.9), channel_id=1, source_target_pairs={{0,2},{1,3},{2,0},{3,1},{4,6},{5,7},{6,4},{7,5},{8,10},{9,11},{10,... | collective-permute-start | bytes 786440 | tf_op jit(solution)/shard_map/ppermute | solution.py:23
  59.8 15.2 %collective-permute-start.3 = (bf16[128,1024]{1,0:T(8,128)(2,1)S(1)}, bf16[128,1024]{1,0:T(8,128)(2,1)}, u32[]{:S(2)}, u32[]{:S(2)}) collective-permute-start(bf16[128,1024]{1,0:T(8,128)(2,1)S(1)} %copy-done.9), channel_id=1, source_target_pairs={{0,3},{1,2},{2,1},{3,0},{4,7},{5,6},{6,5},{7,4},{8,11},{9,10},{10,... | collective-permute-start | bytes 786440 | tf_op jit(solution)/shard_map/ppermute | solution.py:23
  81.4 58.2 %collective-permute-start.19 = (bf16[2,1024,1024]{2,1,0:T(8,128)(2,1)}, bf16[2,1024,1024]{2,1,0:T(8,128)(2,1)}, u32[]{:S(2)}, u32[]{:S(2)}) collective-permute-start(bf16[2,1024,1024]{2,1,0:T(8,128)(2,1)} %shard_map.92), channel_id=1, source_target_pairs={{24,0},{0,8},{8,16},{16,24},{25,1},{1,9},{9,17},{17,25},{26,2},{2,... | collective-permute-start | bytes 12582920 | tf_op jit(solution)/shard_map/ppermute | solution.py:381
  107.2 13.6 %collective-permute-start.14 = (bf16[128,1024]{1,0:T(8,128)(2,1)}, bf16[128,1024]{1,0:T(8,128)(2,1)}, u32[]{:S(2)}, u32[]{:S(2)}) collective-permute-start(bf16[128,1024]{1,0:T(8,128)(2,1)} %get-tuple-element.65), channel_id=1, source_target_pairs={{0,2},{1,3},{2,0},{3,1},{4,6},{5,7},{6,4},{7,5},{8,10},{9,11},{10,... | collective-permute-start | bytes 786440 | tf_op jit(solution)/shard_map/ppermute | solution.py:23
  123.7 13.3 %collective-permute-start.17 = (bf16[128,1024]{1,0:T(8,128)(2,1)S(1)}, bf16[128,1024]{1,0:T(8,128)(2,1)S(1)}, u32[]{:S(2)}, u32[]{:S(2)}) collective-permute-start(bf16[128,1024]{1,0:T(8,128)(2,1)S(1)} %multiply_convert_fusion.1), channel_id=1, source_target_pairs={{0,2},{1,3},{2,0},{3,1},{4,6},{5,7},{6,4},{7,5},{8,10},{9,11},{10,... | collective-permute-start | bytes 786440 | tf_op jit(solution)/shard_map/ppermute | solution.py:23
  137.1 16.8 %collective-permute-start.20 = (bf16[512,1024]{1,0:T(8,128)(2,1)S(1)}, bf16[512,1024]{1,0:T(8,128)(2,1)S(1)}, u32[]{:S(2)}, u32[]{:S(2)}) collective-permute-start(bf16[512,1024]{1,0:T(8,128)(2,1)S(1)} %pad_maximum_fusion.1.refs_2_), channel_id=1, source_target_pairs={{28,4},{4,12},{12,20},{20,28},{29,5},{5,13},{13,21},{21,29},{30,6}... | collective-permute-start | bytes 3145736 | tf_op jit(solution)/shard_map/ppermute | solution.py:381
  155.5 52.5 %collective-permute-start.25 = (bf16[2,1024,1024]{2,1,0:T(8,128)(2,1)}, bf16[2,1024,1024]{2,1,0:T(8,128)(2,1)}, u32[]{:S(2)}, u32[]{:S(2)}) collective-permute-start(bf16[2,1024,1024]{2,1,0:T(8,128)(2,1)} %shard_map.94.refs_1_.refs_2_), channel_id=1, source_target_pairs={{24,0},{0,8},{8,16},{16,24},{25,1},{1,9},{9,17},{17,25},{26,2},{2,... | collective-permute-start | bytes 12582920 | tf_op jit(solution)/shard_map/ppermute | solution.py:381
  163.7 20.4 %collective-permute-start.21 = (bf16[1024,1024]{1,0:T(8,128)(2,1)}, bf16[1024,1024]{1,0:T(8,128)(2,1)}, u32[]{:S(2)}, u32[]{:S(2)}) collective-permute-start(bf16[1024,1024]{1,0:T(8,128)(2,1)} %shard_map.95), channel_id=1, source_target_pairs={{0,4},{8,12},{16,20},{24,28},{1,5},{9,13},{17,21},{25,29},{2,6},{1... | collective-permute-start | bytes 6291464 | tf_op jit(solution)/shard_map/ppermute | solution.py:381
  235.4 13.6 %collective-permute-start.30 = (bf16[128,1024]{1,0:T(8,128)(2,1)S(1)}, bf16[128,1024]{1,0:T(8,128)(2,1)S(1)}, u32[]{:S(2)}, u32[]{:S(2)}) collective-permute-start(bf16[128,1024]{1,0:T(8,128)(2,1)S(1)} %multiply_convert_fusion.refs_2_), channel_id=1, source_target_pairs={{0,2},{1,3},{2,0},{3,1},{4,6},{5,7},{6,4},{7,5},{8,10},{9,11},{10,... | collective-permute-start | bytes 786440 | tf_op jit(solution)/shard_map/ppermute | solution.py:23
  271.0 14.0 %collective-permute-start.34 = (bf16[256,1024]{1,0:T(8,128)(2,1)S(1)}, bf16[256,1024]{1,0:T(8,128)(2,1)S(1)}, u32[]{:S(2)}, u32[]{:S(2)}) collective-permute-start(bf16[256,1024]{1,0:T(8,128)(2,1)S(1)} %get-tuple-element.100), channel_id=1, source_target_pairs={{0,8},{4,12},{24,16},{28,20},{1,9},{5,13},{25,17},{29,21},{2,10},{... | collective-permute-start | bytes 1572872 | tf_op jit(solution)/shard_map/ppermute | solution.py:316
  272.8 23.4 %collective-permute-start.42 = (bf16[256,1024]{1,0:T(8,128)(2,1)S(1)}, bf16[256,1024]{1,0:T(8,128)(2,1)}, u32[]{:S(2)}, u32[]{:S(2)}) collective-permute-start(bf16[256,1024]{1,0:T(8,128)(2,1)S(1)} %get-tuple-element.99), channel_id=1, source_target_pairs={{0,8},{4,12},{24,16},{28,20},{1,9},{5,13},{25,17},{29,21},{2,10},{... | collective-permute-start | bytes 1572872 | tf_op jit(solution)/shard_map/ppermute | solution.py:316
  285.2 13.0 %collective-permute-start.35 = (bf16[256,1024]{1,0:T(8,128)(2,1)S(1)}, bf16[256,1024]{1,0:T(8,128)(2,1)}, u32[]{:S(2)}, u32[]{:S(2)}) collective-permute-start(bf16[256,1024]{1,0:T(8,128)(2,1)S(1)} %fusion), channel_id=1, source_target_pairs={{8,16},{12,20},{16,8},{20,12},{9,17},{13,21},{17,9},{21,13},{10,18... | collective-permute-start | bytes 1572872 | tf_op jit(solution)/shard_map/ppermute | solution.py:316
  286.7 21.0 %collective-permute-start.39 = (bf16[256,1024]{1,0:T(8,128)(2,1)S(1)}, bf16[256,1024]{1,0:T(8,128)(2,1)S(1)}, u32[]{:S(2)}, u32[]{:S(2)}) collective-permute-start(bf16[256,1024]{1,0:T(8,128)(2,1)S(1)} %get-tuple-element.104), channel_id=1, source_target_pairs={{0,8},{4,12},{24,16},{28,20},{1,9},{5,13},{25,17},{29,21},{2,10},{... | collective-permute-start | bytes 1572872 | tf_op jit(solution)/shard_map/ppermute | solution.py:316
  300.2 17.8 %collective-permute-start.36 = (bf16[256,1024]{1,0:T(8,128)(2,1)}, bf16[256,1024]{1,0:T(8,128)(2,1)S(1)}, u32[]{:S(2)}, u32[]{:S(2)}) collective-permute-start(bf16[256,1024]{1,0:T(8,128)(2,1)} %shard_map.103), channel_id=1, source_target_pairs={{0,8},{4,12},{24,16},{28,20},{1,9},{5,13},{25,17},{29,21},{2,10},{... | collective-permute-start | bytes 1572872 | tf_op jit(solution)/shard_map/ppermute | solution.py:316
  307.9 20.2 %collective-permute-start.40 = (bf16[256,1024]{1,0:T(8,128)(2,1)S(1)}, bf16[256,1024]{1,0:T(8,128)(2,1)S(1)}, u32[]{:S(2)}, u32[]{:S(2)}) collective-permute-start(bf16[256,1024]{1,0:T(8,128)(2,1)S(1)} %fusion.4), channel_id=1, source_target_pairs={{8,16},{12,20},{16,8},{20,12},{9,17},{13,21},{17,9},{21,13},{10,18... | collective-permute-start | bytes 1572872 | tf_op jit(solution)/shard_map/ppermute | solution.py:316
  308.6 19.4 %collective-permute-start.45 = (bf16[256,1024]{1,0:T(8,128)(2,1)}, bf16[256,1024]{1,0:T(8,128)(2,1)S(1)}, u32[]{:S(2)}, u32[]{:S(2)}) collective-permute-start(bf16[256,1024]{1,0:T(8,128)(2,1)} %fusion.1.refs_1_), channel_id=1, source_target_pairs={{8,0},{12,4},{16,24},{20,28},{9,1},{13,5},{17,25},{21,29},{10,2},{... | collective-permute-start | bytes 1572872 | tf_op jit(solution)/shard_map/ppermute | solution.py:316
  310.1 29.1 %collective-permute-start.44 = (bf16[256,1024]{1,0:T(8,128)(2,1)S(1)}, bf16[256,1024]{1,0:T(8,128)(2,1)S(1)}, u32[]{:S(2)}, u32[]{:S(2)}) collective-permute-start(bf16[256,1024]{1,0:T(8,128)(2,1)S(1)} %fusion.7), channel_id=1, source_target_pairs={{8,0},{12,4},{16,24},{20,28},{9,1},{13,5},{17,25},{21,29},{10,2},{... | collective-permute-start | bytes 1572872 | tf_op jit(solution)/shard_map/ppermute | solution.py:316
  319.5 25.5 %collective-permute-start.37 = (bf16[256,1024]{1,0:T(8,128)(2,1)S(1)}, bf16[256,1024]{1,0:T(8,128)(2,1)S(1)}, u32[]{:S(2)}, u32[]{:S(2)}) collective-permute-start(bf16[256,1024]{1,0:T(8,128)(2,1)S(1)} %fusion.2), channel_id=1, source_target_pairs={{8,16},{12,20},{16,8},{20,12},{9,17},{13,21},{17,9},{21,13},{10,18... | collective-permute-start | bytes 1572872 | tf_op jit(solution)/shard_map/ppermute | solution.py:316
  328.3 19.6 %collective-permute-start.41 = (bf16[256,1024]{1,0:T(8,128)(2,1)S(1)}, bf16[256,1024]{1,0:T(8,128)(2,1)S(1)}, u32[]{:S(2)}, u32[]{:S(2)}) collective-permute-start(bf16[256,1024]{1,0:T(8,128)(2,1)S(1)} %fusion.5), channel_id=1, source_target_pairs={{8,0},{12,4},{16,24},{20,28},{9,1},{13,5},{17,25},{21,29},{10,2},{... | collective-permute-start | bytes 1572872 | tf_op jit(solution)/shard_map/ppermute | solution.py:316
  345.2 16.2 %collective-permute-start.38 = (bf16[256,1024]{1,0:T(8,128)(2,1)S(1)}, bf16[256,1024]{1,0:T(8,128)(2,1)S(1)}, u32[]{:S(2)}, u32[]{:S(2)}) collective-permute-start(bf16[256,1024]{1,0:T(8,128)(2,1)S(1)} %fusion.3), channel_id=1, source_target_pairs={{8,0},{12,4},{16,24},{20,28},{9,1},{13,5},{17,25},{21,29},{10,2},{... | collective-permute-start | bytes 1572872 | tf_op jit(solution)/shard_map/ppermute | solution.py:316
  (47 other events, 402.0 us)
